TPU v7x, 256 devices: a whole 4x4x8 slice. The times are simulated.
256 devices in a mesh: doc: 32 (over y, z), tok: 8 (over x, core).
Axes of the slice: x: 4, y: 4, z: 8, core: 2. Of those that a mesh axis runs over, the one named last changes fastest.
Arguments:
- query_states: bfloat16 [256, 32, 1024], P('doc', 'tok'), may hold values from -6 to 6
- proj_weight: bfloat16 [1024, 128], replicated, may hold values from -0.1875 to 0.1875
- doc_vectors: bfloat16 [32768, 128, 128], P('doc', 'tok'), may hold values from -0.52734375 to 0.52734375
- document_token_length: int32 [32768], P('doc'), may hold values from 1 to 128
- candidates: int32 [256, 256], P('doc'), may hold values from 0 to 32767, as said below
Outputs:
- scores: float32 [256, 256], P('doc')
Inputs may be any that keep to these rules, and one draw needn't show every extreme that they name: `candidates`: write shard(e) = id // 1024. Among the 2048 entries of the queries held at one position along doc, one shard, the same for every index of doc, is named by exactly 128 entries, and each other shard by the floor or the ceiling of 1920 / 31 entries. Ids may repeat within a query.
All inputs are finite; a program needn't handle non-finite values.
Results may differ from a plain program's by a relative error of at most 0.0003.
Values may be sent and summed in bfloat16 or wider, within the bound.
A program may use at most 64 MiB of HBM per device.

v0:
```python
import math

import jax
import jax.numpy as jnp
from jax import lax
from jax.sharding import PartitionSpec as P


def owner_ranks(flat_shard, shard_count):
    onehot = (flat_shard[:, None] == jnp.arange(shard_count, dtype=jnp.int32)[None, :]).astype(
        jnp.int32
    )
    return jnp.sum(jnp.cumsum(onehot, axis=0) * onehot, axis=1) - 1


def on_device(query_states, proj_weight, doc_vectors, document_token_length, candidates):
    owner_grouped, cand_count = candidates.shape
    shard_count = lax.axis_size("doc")
    doc_local, slot_local, vec_width = doc_vectors.shape
    capacity = 2 * owner_grouped * cand_count // shard_count
    total_slots = shard_count * capacity
    proj = jnp.einsum("qtd,de->qte", query_states, proj_weight, preferred_element_type=jnp.float32)
    unit = (proj * lax.rsqrt(jnp.sum(proj * proj, axis=-1, keepdims=True) + 1e-06)).astype(
        jnp.bfloat16
    )
    owner_whole = lax.all_gather(unit, "tok", axis=1, tiled=True)
    every_query = lax.all_gather(owner_whole, "doc", axis=0, tiled=True)
    query_tokens = every_query.shape[1]
    flat_cands = candidates.reshape(-1)
    flat_shard = flat_cands // doc_local
    flat_rank = owner_ranks(flat_shard, shard_count)
    my_shard = lax.axis_index("doc")
    query_global = (
        my_shard * owner_grouped
        + jnp.arange(owner_grouped * cand_count, dtype=jnp.int32) // cand_count
    )
    send_query = (
        jnp.zeros((shard_count, capacity), jnp.int32).at[flat_shard, flat_rank].set(query_global)
    )
    send_doc = (
        jnp.zeros((shard_count, capacity), jnp.int32)
        .at[flat_shard, flat_rank]
        .set(flat_cands % doc_local)
    )
    slot_query, slot_doc = (
        lax.all_to_all(send_query, "doc", split_axis=0, concat_axis=0, tiled=True),
        lax.all_to_all(send_doc, "doc", split_axis=0, concat_axis=0, tiled=True),
    )
    group_size = math.gcd(shard_count, max(1, 512 // capacity))
    step_count = shard_count // group_size
    owner_queries = every_query.reshape(
        step_count, group_size, owner_grouped * query_tokens, vec_width
    )
    query_local = (slot_query % owner_grouped).reshape(step_count, group_size, capacity)
    doc_groups = slot_doc.reshape(step_count, group_size, capacity)
    tok_positions = lax.axis_index("tok") * slot_local + jnp.arange(slot_local, dtype=jnp.int32)
    query_slots = jnp.arange(owner_grouped, dtype=jnp.int32)

    def block_maxima(triple):
        query_block, local_block, doc_block = triple
        document_matrices = doc_vectors[doc_block]
        live = tok_positions[None, None, :] < document_token_length[doc_block][:, :, None]
        similarity_scores = jnp.einsum(
            "gcki,gri->gckr", document_matrices, query_block, preferred_element_type=jnp.float32
        )
        similarity_scores = jnp.where(live[:, :, :, None], similarity_scores, jnp.float32(-1e30))
        token_best = jnp.max(similarity_scores, axis=2).reshape(
            group_size, capacity, owner_grouped, query_tokens
        )
        picked = local_block[:, :, None] == query_slots[None, None, :]
        return jnp.sum(jnp.where(picked[:, :, :, None], token_best, jnp.float32(0.0)), axis=2)

    partial_value = lax.map(block_maxima, (owner_queries, query_local, doc_groups))
    partial_value = partial_value.reshape(total_slots, query_tokens)
    merged = lax.pmax(partial_value, "tok")
    slot_scores = jnp.sum(merged, axis=1)
    returned = lax.all_to_all(
        slot_scores.reshape(shard_count, capacity), "doc", split_axis=0, concat_axis=0, tiled=True
    )
    return returned[flat_shard, flat_rank].reshape(owner_grouped, cand_count)


def solution(mesh):
    placed = (P("doc", "tok", None), P(), P("doc", "tok", None), P("doc"), P("doc", None))
    return jax.shard_map(
        on_device, mesh=mesh, in_specs=placed, out_specs=P("doc", None), check_vma=False
    )
```

profile of v0, /device:TPU:1, one launch (start us, length us, event | category | flops | bytes accessed | tf_op | source)
XLA Modules:
  0.0 278.6 jit_solution(9781640307714994140)
XLA Ops:
  8.7 15.8 %all_gather.6 = bf16[8,32,128]{2,0,1:T(8,128)(2,1)S(1)} all-gather(bf16[8,4,128]{2,0,1:T(8,128)(2,1)S(1)} %copy.30), channel_id=1, replica_groups=mesh['doc'=32,'tok'=8] {'tok'}, dimensions={1}, use_global_device_ids=true | all-gather | bytes 73728 | tf_op jit(solution)/shard_map/all_gather | solution.py:26
  25.9 9.1 %reduce-window.6 = s32[32,16,128]{2,1,0:T(8,128)S(1)} reduce-window(s32[32,16,128]{2,1,0:T(8,128)S(1)} %fusion.13, s32[]{:T(128)} %copy.61), window={size=1x1x128 pad=0_0x0_0x127_0}, to_apply=%region_1.2 | reduce-window | flops 8323072 | bytes 524292 | tf_op jit(solution)/shard_map/reduce-window
  36.2 8.6 %scatter_custom_fusion = s32[4096]{0:T(1024)} fusion(s32[2048]{0:T(1024)S(1)} %get-tuple-element.99, s32[2048]{0:T(1024)S(1)} %get-tuple-element.98, s32[]{:T(128)} %copy.61), kind=kCustom, calls=%fused_computation.65 | custom fusion | bytes 16388
  44.8 9.8 %all-to-all-start = ((s32[32,1,128]{2,1,0:T(1,128)}), s32[32,1,128]{2,1,0:T(1,128)S(1)}, u32[]{:S(2)}, u32[]{:S(2)}) async-start(s32[32,1,128]{2,1,0:T(1,128)} %bitcast.5), calls=%async_computation | async-start | bytes 32768 | tf_op jit(solution)/shard_map/all_to_all | solution.py:46
  54.6 8.6 %scatter_custom_fusion.1 = s32[4096]{0:T(1024)} fusion(s32[2048]{0:T(1024)S(1)} %get-tuple-element.99, s32[2048]{0:T(1024)S(1)} %get-tuple-element.92, s32[]{:T(128)} %copy.61), kind=kCustom, calls=%fused_computation.63 | custom fusion | bytes 16388
  63.3 9.2 %all-to-all-start.1 = ((s32[32,1,128]{2,1,0:T(1,128)}), s32[32,1,128]{2,1,0:T(1,128)S(1)}, u32[]{:S(2)}, u32[]{:S(2)}) async-start(s32[32,1,128]{2,1,0:T(1,128)} %bitcast.7), calls=%async_computation.1 | async-start | bytes 32768 | tf_op jit(solution)/shard_map/all_to_all | solution.py:47
  72.6 8.6 %all-to-all-done.1 = s32[32,1,128]{2,1,0:T(1,128)S(1)} async-done(((s32[32,1,128]{2,1,0:T(1,128)}), s32[32,1,128]{2,1,0:T(1,128)S(1)}, u32[]{:S(2)}, u32[]{:S(2)}) %all-to-all-start.1) | async-done | bytes 16416 | tf_op jit(solution)/shard_map/all_to_all | solution.py:47
  81.1 18.7 %all-gather.2.cloned.1.call-done = bf16[256,32,128]{2,1,0:T(8,128)(2,1)} async-done(((bf16[8,32,128]{2,1,0:T(8,128)(2,1)}), bf16[256,32,128]{2,1,0:T(8,128)(2,1)}) %all-gather.2.cloned.1.call-update) | async-done | bytes 2097168 | tf_op jit(solution)/shard_map/all_gather | solution.py:27
  99.8 72.8 %while.11 = (s32[]{:T(128)}, f32[8,4,128,32]{2,1,0,3:T(4,128)S(1)}, s32[8,4,128]{2,1,0:T(4,128)S(1)}, s32[8,4,128]{2,1,0:T(4,128)S(1)}, s32[1024]{0:T(1024)S(1)}...) while((s32[]{:T(128)}, f32[8,4,128,32]{2,1,0,3:T(4,128)S(1)}, ...), condition=%wide.region_9.10_spmd.clone, body=%wide.region_6.9_spmd.clone.sunk | while | flops 541194752 | bytes 8899309 | solution.py:73
  102.2 3.4 %gather_fusion.1 = bf16[512,16,128]{2,1,0:T(8,128)(2,1)S(1)} fusion(bf16[1024,16,128]{2,1,0:T(8,128)(2,1)} %get-tuple-element.172, s32[1024]{0:T(1024)S(1)} %pad_clamp_fusion.2), kind=kCustom, calls=%fused_computation.1.clone.clone.1 | custom fusion | bytes 4196352 | tf_op jit(solution)/shard_map/while/body/eval_jaxpr/gather | solution.py:61
  105.6 2.9 %select_reduce_fusion.4 = f32[4,128,256]{2,1,0:T(8,128)S(1)} fusion(pred[4,128,16]{1,2,0:T(8,128)(4,1)S(1)} %broadcast_compare_fusion.2, bf16[4,128,16,128]{3,2,1,0:T(8,128)(2,1)S(1)} %bitcast.75, bf16[8,4,256,128]{3,2,1,0:T(8,128)(2,1)} %get-tuple-element.173, s32[]{:T(128)} %get-tuple-element.158), kind=kOutput, calls=%fused_computation.7.clone.1 | convolution fusion | flops 540934144 | bytes 2892288 | tf_op jit(solution)/shard_map/while/body/eval_jaxpr/gcki,gri->gckr/dot_general | solution.py:63
  108.9 2.3 gather_fusion
  111.3 3.4 %gather_fusion.1 = bf16[512,16,128]{2,1,0:T(8,128)(2,1)S(1)} fusion(bf16[1024,16,128]{2,1,0:T(8,128)(2,1)} %get-tuple-element.172, s32[1024]{0:T(1024)S(1)} %pad_clamp_fusion.2), kind=kCustom, calls=%fused_computation.1.clone.clone.1 | custom fusion | bytes 4196352 | tf_op jit(solution)/shard_map/while/body/eval_jaxpr/gather | solution.py:61
  114.7 2.9 %select_reduce_fusion.4 = f32[4,128,256]{2,1,0:T(8,128)S(1)} fusion(pred[4,128,16]{1,2,0:T(8,128)(4,1)S(1)} %broadcast_compare_fusion.2, bf16[4,128,16,128]{3,2,1,0:T(8,128)(2,1)S(1)} %bitcast.75, bf16[8,4,256,128]{3,2,1,0:T(8,128)(2,1)} %get-tuple-element.173, s32[]{:T(128)} %get-tuple-element.158), kind=kOutput, calls=%fused_computation.7.clone.1 | convolution fusion | flops 540934144 | bytes 2892288 | tf_op jit(solution)/shard_map/while/body/eval_jaxpr/gcki,gri->gckr/dot_general | solution.py:63
  118.0 2.3 gather_fusion
  120.4 3.4 %gather_fusion.1 = bf16[512,16,128]{2,1,0:T(8,128)(2,1)S(1)} fusion(bf16[1024,16,128]{2,1,0:T(8,128)(2,1)} %get-tuple-element.172, s32[1024]{0:T(1024)S(1)} %pad_clamp_fusion.2), kind=kCustom, calls=%fused_computation.1.clone.clone.1 | custom fusion | bytes 4196352 | tf_op jit(solution)/shard_map/while/body/eval_jaxpr/gather | solution.py:61
  123.8 2.9 %select_reduce_fusion.4 = f32[4,128,256]{2,1,0:T(8,128)S(1)} fusion(pred[4,128,16]{1,2,0:T(8,128)(4,1)S(1)} %broadcast_compare_fusion.2, bf16[4,128,16,128]{3,2,1,0:T(8,128)(2,1)S(1)} %bitcast.75, bf16[8,4,256,128]{3,2,1,0:T(8,128)(2,1)} %get-tuple-element.173, s32[]{:T(128)} %get-tuple-element.158), kind=kOutput, calls=%fused_computation.7.clone.1 | convolution fusion | flops 540934144 | bytes 2892288 | tf_op jit(solution)/shard_map/while/body/eval_jaxpr/gcki,gri->gckr/dot_general | solution.py:63
  127.1 2.3 gather_fusion
  129.5 3.4 %gather_fusion.1 = bf16[512,16,128]{2,1,0:T(8,128)(2,1)S(1)} fusion(bf16[1024,16,128]{2,1,0:T(8,128)(2,1)} %get-tuple-element.172, s32[1024]{0:T(1024)S(1)} %pad_clamp_fusion.2), kind=kCustom, calls=%fused_computation.1.clone.clone.1 | custom fusion | bytes 4196352 | tf_op jit(solution)/shard_map/while/body/eval_jaxpr/gather | solution.py:61
  132.9 2.9 %select_reduce_fusion.4 = f32[4,128,256]{2,1,0:T(8,128)S(1)} fusion(pred[4,128,16]{1,2,0:T(8,128)(4,1)S(1)} %broadcast_compare_fusion.2, bf16[4,128,16,128]{3,2,1,0:T(8,128)(2,1)S(1)} %bitcast.75, bf16[8,4,256,128]{3,2,1,0:T(8,128)(2,1)} %get-tuple-element.173, s32[]{:T(128)} %get-tuple-element.158), kind=kOutput, calls=%fused_computation.7.clone.1 | convolution fusion | flops 540934144 | bytes 2892288 | tf_op jit(solution)/shard_map/while/body/eval_jaxpr/gcki,gri->gckr/dot_general | solution.py:63
  136.2 2.3 gather_fusion
  138.6 3.4 %gather_fusion.1 = bf16[512,16,128]{2,1,0:T(8,128)(2,1)S(1)} fusion(bf16[1024,16,128]{2,1,0:T(8,128)(2,1)} %get-tuple-element.172, s32[1024]{0:T(1024)S(1)} %pad_clamp_fusion.2), kind=kCustom, calls=%fused_computation.1.clone.clone.1 | custom fusion | bytes 4196352 | tf_op jit(solution)/shard_map/while/body/eval_jaxpr/gather | solution.py:61
  142.0 2.9 %select_reduce_fusion.4 = f32[4,128,256]{2,1,0:T(8,128)S(1)} fusion(pred[4,128,16]{1,2,0:T(8,128)(4,1)S(1)} %broadcast_compare_fusion.2, bf16[4,128,16,128]{3,2,1,0:T(8,128)(2,1)S(1)} %bitcast.75, bf16[8,4,256,128]{3,2,1,0:T(8,128)(2,1)} %get-tuple-element.173, s32[]{:T(128)} %get-tuple-element.158), kind=kOutput, calls=%fused_computation.7.clone.1 | convolution fusion | flops 540934144 | bytes 2892288 | tf_op jit(solution)/shard_map/while/body/eval_jaxpr/gcki,gri->gckr/dot_general | solution.py:63
  147.7 3.4 %gather_fusion.1 = bf16[512,16,128]{2,1,0:T(8,128)(2,1)S(1)} fusion(bf16[1024,16,128]{2,1,0:T(8,128)(2,1)} %get-tuple-element.172, s32[1024]{0:T(1024)S(1)} %pad_clamp_fusion.2), kind=kCustom, calls=%fused_computation.1.clone.clone.1 | custom fusion | bytes 4196352 | tf_op jit(solution)/shard_map/while/body/eval_jaxpr/gather | solution.py:61
  151.1 2.9 %select_reduce_fusion.4 = f32[4,128,256]{2,1,0:T(8,128)S(1)} fusion(pred[4,128,16]{1,2,0:T(8,128)(4,1)S(1)} %broadcast_compare_fusion.2, bf16[4,128,16,128]{3,2,1,0:T(8,128)(2,1)S(1)} %bitcast.75, bf16[8,4,256,128]{3,2,1,0:T(8,128)(2,1)} %get-tuple-element.173, s32[]{:T(128)} %get-tuple-element.158), kind=kOutput, calls=%fused_computation.7.clone.1 | convolution fusion | flops 540934144 | bytes 2892288 | tf_op jit(solution)/shard_map/while/body/eval_jaxpr/gcki,gri->gckr/dot_general | solution.py:63
  156.8 3.4 %gather_fusion.1 = bf16[512,16,128]{2,1,0:T(8,128)(2,1)S(1)} fusion(bf16[1024,16,128]{2,1,0:T(8,128)(2,1)} %get-tuple-element.172, s32[1024]{0:T(1024)S(1)} %pad_clamp_fusion.2), kind=kCustom, calls=%fused_computation.1.clone.clone.1 | custom fusion | bytes 4196352 | tf_op jit(solution)/shard_map/while/body/eval_jaxpr/gather | solution.py:61
  160.2 2.9 %select_reduce_fusion.4 = f32[4,128,256]{2,1,0:T(8,128)S(1)} fusion(pred[4,128,16]{1,2,0:T(8,128)(4,1)S(1)} %broadcast_compare_fusion.2, bf16[4,128,16,128]{3,2,1,0:T(8,128)(2,1)S(1)} %bitcast.75, bf16[8,4,256,128]{3,2,1,0:T(8,128)(2,1)} %get-tuple-element.173, s32[]{:T(128)} %get-tuple-element.158), kind=kOutput, calls=%fused_computation.7.clone.1 | convolution fusion | flops 540934144 | bytes 2892288 | tf_op jit(solution)/shard_map/while/body/eval_jaxpr/gcki,gri->gckr/dot_general | solution.py:63
  165.9 3.4 %gather_fusion.1 = bf16[512,16,128]{2,1,0:T(8,128)(2,1)S(1)} fusion(bf16[1024,16,128]{2,1,0:T(8,128)(2,1)} %get-tuple-element.172, s32[1024]{0:T(1024)S(1)} %pad_clamp_fusion.2), kind=kCustom, calls=%fused_computation.1.clone.clone.1 | custom fusion | bytes 4196352 | tf_op jit(solution)/shard_map/while/body/eval_jaxpr/gather | solution.py:61
  169.3 2.9 %select_reduce_fusion.4 = f32[4,128,256]{2,1,0:T(8,128)S(1)} fusion(pred[4,128,16]{1,2,0:T(8,128)(4,1)S(1)} %broadcast_compare_fusion.2, bf16[4,128,16,128]{3,2,1,0:T(8,128)(2,1)S(1)} %bitcast.75, bf16[8,4,256,128]{3,2,1,0:T(8,128)(2,1)} %get-tuple-element.173, s32[]{:T(128)} %get-tuple-element.158), kind=kOutput, calls=%fused_computation.7.clone.1 | convolution fusion | flops 540934144 | bytes 2892288 | tf_op jit(solution)/shard_map/while/body/eval_jaxpr/gcki,gri->gckr/dot_general | solution.py:63
  173.6 65.3 %all-reduce.2.cloned.1.call-done = f32[4096,32]{0,1:T(8,128)} async-done(((f32[4096,32]{0,1:T(8,128)}), f32[4096,32]{0,1:T(8,128)}) %all-reduce.2.cloned.1.call-update) | async-done | bytes 524304 | tf_op jit(solution)/shard_map/pmax | solution.py:75
  240.1 18.0 %all_to_all.33 = f32[32,1,128]{2,1,0:T(1,128)S(1)} all-to-all(f32[32,1,128]{2,1,0:T(1,128)S(1)} %bitcast.82), channel_id=1, replica_groups=mesh['doc'=32,'tok'=8] {'doc'}, dimensions={0} | all-to-all | bytes 32768 | tf_op jit(solution)/shard_map/all_to_all | solution.py:77
  258.1 13.1 %gather_fusion.2 = f32[2048]{0:T(1024)S(1)} fusion(f32[32,128]{1,0:T(8,128)S(1)} %bitcast.72, s32[2048]{0:T(1024)S(1)} %bitcast.73), kind=kCustom, calls=%fused_computation.2 | custom fusion | bytes 32768 | tf_op jit(solution)/shard_map/gather | solution.py:80
  (117 shorter events, 19.9 us)
Async XLA Ops:
  6.5 1.0 copy-start
  6.5 29.4 %copy-start.4 = (s32[2]{0:T(128)S(1)}, s32[2]{0:T(128)}, u32[]{:S(2)}) copy-start(s32[2]{0:T(128)} %constant.107) | copy-start | bytes 28
  6.5 29.5 %copy-start.3 = (s32[2]{0:T(128)S(1)}, s32[2]{0:T(128)}, u32[]{:S(2)}) copy-start(s32[2]{0:T(128)} %constant.110) | copy-start | bytes 28
  6.5 29.0 %copy-start.2 = (s32[8,256]{1,0:T(8,128)S(1)}, s32[8,256]{1,0:T(8,128)}, u32[]{:S(2)}) copy-start(s32[8,256]{1,0:T(8,128)} %param.11) | copy-start | bytes 24580
  6.5 93.3 %copy-start.1 = (s32[1024]{0:T(1024)S(1)}, s32[1024]{0:T(1024)}, u32[]{:S(2)}) copy-start(s32[1024]{0:T(1024)} %param.10) | copy-start | bytes 12292
  6.5 93.3 %all-gather.2.cloned.1.call-start = ((), (), s32[]{:S(2)}) async-start(), calls=%async_computation.3 | async-start | bytes 2162688 | tf_op jit(solution)/shard_map/all_gather | solution.py:27
  44.8 18.5 %all-to-all-start = ((s32[32,1,128]{2,1,0:T(1,128)}), s32[32,1,128]{2,1,0:T(1,128)S(1)}, u32[]{:S(2)}, u32[]{:S(2)}) async-start(s32[32,1,128]{2,1,0:T(1,128)} %bitcast.5), calls=%async_computation | async-start | bytes 32768 | tf_op jit(solution)/shard_map/all_to_all | solution.py:46
  63.3 17.9 %all-to-all-start.1 = ((s32[32,1,128]{2,1,0:T(1,128)}), s32[32,1,128]{2,1,0:T(1,128)S(1)}, u32[]{:S(2)}, u32[]{:S(2)}) async-start(s32[32,1,128]{2,1,0:T(1,128)} %bitcast.7), calls=%async_computation.1 | async-start | bytes 32768 | tf_op jit(solution)/shard_map/all_to_all | solution.py:47
  72.5 166.5 %all-reduce.2.cloned.1.call-start = ((), (), s32[]{:S(2)}) async-start(), calls=%async_computation.4 | async-start | bytes 1048576 | tf_op jit(solution)/shard_map/pmax | solution.py:75
Sparse Core Ops, SparseCore 0:
  25.3 74.4 all-gather.1
  173.8 65.1 all-reduce.1
where the time goes:
time: 281 us; the launch traced here: 279 us
  waiting for transfers between devices  92.6 us (33%)
  local copies, waits for them, and re-layouts  82 us (29%)
  blocking collectives  33.8 us (12%)
  matrix products  24.4 us (9%)
  starting transfers between devices  19.1 us (7%)
  between operations  13.6 us (5%)
  other arithmetic  12.3 us (4%)
    pmax x1, waiting for transfers between devices, on_device(): merged = lax.pmax(partial_value, 'tok')  65.3 us
    gather x8, local copies, waits for them, and re-layouts, block_maxima(): document_matrices = doc_vectors[doc_block]  27 us
    dot_general x8, matrix products, block_maxima(): jnp.einsum('gcki,gri->gckr', document_matrices, query_block, preferred_el...  23.3 us
    all_gather x1, waiting for transfers between devices, on_device(): every_query = lax.all_gather(owner_whole, 'doc', axis=0, tiled=True)  18.7 us
    gather x8, local copies, waits for them, and re-layouts, block_maxima(): document_token_length[doc_block][:, :, None]  18.3 us
    unnamed x14, local copies, waits for them, and re-layouts  18.2 us
    all_to_all x1, blocking collectives, on_device(): lax.all_to_all(slot_scores.reshape(shard_count, capacity), 'doc', split_a...  18 us
    all_gather x1, blocking collectives, on_device(): owner_whole = lax.all_gather(unit, 'tok', axis=1, tiled=True)  15.8 us
  transfers between devices with their start and end apart: 4, of which 3 were waited for; matrix products, arithmetic and copies ran while one was open for 10% of the time, Pallas kernels for 0%

commit v1 on v0

v1 whole, which is shorter than its diff:
```python
import functools

import jax
import jax.numpy as jnp
from jax import lax
from jax.experimental import pallas as pl
from jax.experimental.pallas import tpu as pltpu
from jax.sharding import PartitionSpec as P

MESH = pl.DeviceIdType.MESH
F32, BF16, I32 = jnp.float32, jnp.bfloat16, jnp.int32
NT = (((1,), (1,)), ((), ()))
AHEAD = 8


def iota(shape, dim):
    return lax.broadcasted_iota(I32, shape, dim)


def kernel(
    ny, nz, nt, docs_hbm, qs_hbm, w_hbm, len_ref, cand_ref, out_ref,
    docs, qs, w, ublk, qall, lists_out, lists_in, lists, expand, lens_in, onehots, ranks,
    best, inbox, sums, table, table2,
    in_sem, a_send, a_recv, l_send, l_recv, q_recv, y_send, zp_send, zm_send, sib_send,
    m_send, m_recv, t_send, t_recv, s_sem,
):
    no = ny * nz
    d, t = lax.axis_index("doc"), lax.axis_index("tok")
    y, z, c = d // nz, d % nz, t % 2
    sibling = t + 1 - 2 * c
    nq, cands = cand_ref.shape
    ndocs = docs.shape[0]
    slots = docs.shape[1]
    shift = ndocs.bit_length() - 1
    qrows = nq * (ublk.shape[1] // nq) * nt
    cap = lists_in.shape[2]

    loads = [
        pltpu.make_async_copy(src, dst, in_sem.at[i])
        for i, (src, dst) in enumerate(((qs_hbm, qs), (w_hbm, w), (docs_hbm, docs)))
    ]
    for load in loads:
        load.start()

    barrier = pltpu.get_barrier_semaphore()

    def greet_tok(p, carry):
        pl.semaphore_signal(barrier, inc=1, device_id={"doc": d, "tok": (t + p) % nt}, device_id_type=MESH)
        return carry

    def greet_doc(p, carry):
        pl.semaphore_signal(barrier, inc=1, device_id={"doc": (d + p) % no, "tok": t}, device_id_type=MESH)
        return carry

    lax.fori_loop(1, nt, greet_tok, 0)
    lax.fori_loop(1, no, greet_doc, 0)

    def send(src, dst, ssem, rsem, doc, tok):
        return pltpu.make_async_remote_copy(
            src_ref=src, dst_ref=dst, send_sem=ssem, recv_sem=rsem,
            device_id={"doc": doc, "tok": tok}, device_id_type=MESH,
        )

    cand = cand_ref[...]
    shard_rows = []
    for q in range(nq):
        shard_rows.append((iota((no, cands), 0) == (cand[q : q + 1] >> shift)).astype(F32))
    before = (iota((cands, cands), 0) < iota((cands, cands), 1)).astype(BF16)
    prefix = jnp.dot(
        jnp.concatenate(shard_rows, axis=0).astype(BF16), before, preferred_element_type=F32
    )
    base = jnp.zeros((no, 1), F32)
    coded = jnp.zeros((2 * no, cap), F32)
    for q in range(nq):
        mine = shard_rows[q]
        rank = jnp.sum(mine * (prefix[no * q : no * (q + 1)] + base), axis=0, keepdims=True)
        base = base + jnp.sum(mine, axis=1, keepdims=True)
        ranks[q] = rank
        onehots[q] = mine.astype(BF16)
        local = cand[q : q + 1] & (ndocs - 1)
        high = (local >> 8) + (ndocs >> 8) * q
        low = local & 255
        rank_rows = (iota((cap, cands), 0).astype(F32) == rank).astype(BF16)
        lhs = jnp.concatenate([mine * high.astype(F32), mine * low.astype(F32)], axis=0)
        coded = coded + lax.dot_general(lhs.astype(BF16), rank_rows, NT, preferred_element_type=F32)
    packed = coded[:no].astype(I32) * 256 + coded[no:].astype(I32)
    for s in range(no):
        lists_out[s] = packed[s : s + 1]
    lists_in[d] = lists_out[d]

    loads[0].wait()
    loads[1].wait()
    proj = jnp.dot(qs[...], w[...], preferred_element_type=F32)
    unit = proj * lax.rsqrt(jnp.sum(proj * proj, axis=-1, keepdims=True) + 1e-06)
    ublk[t] = unit.astype(BF16)

    pl.semaphore_wait(barrier, nt - 1 + no - 1)

    def send_unit(p):
        return send(ublk.at[t], ublk.at[t], a_send.at[p], a_recv.at[t], d, (t + p) % nt)

    def send_list(p):
        s = (d + p) % no
        return send(lists_out.at[s], lists_in.at[d], l_send.at[p], l_recv.at[d], s, t)

    def start_of(make):
        def body(p, carry):
            make(p).start()
            return carry

        return body

    def sent_of(make):
        def body(p, carry):
            make(p).wait_send()
            return carry

        return body

    lax.fori_loop(1, nt, start_of(send_unit), 0)
    lax.fori_loop(1, no, start_of(send_list), 0)

    def unit_arrived(p, carry):
        src = (t + p) % nt
        send(ublk.at[src], ublk.at[src], a_send.at[0], a_recv.at[src], d, src).wait_recv()
        return carry

    lax.fori_loop(1, nt, unit_arrived, 0)

    per = ublk.shape[1] // nq
    row, col = iota((qrows, qrows), 0), iota((qrows, qrows), 1)
    from_row = ((row // per) % nt) * (per * nq) + (row // (per * nt)) * per + row % per
    order = (from_row == col).astype(BF16)
    mixed = jnp.concatenate([ublk[i] for i in range(nt)], axis=0)
    sorted_rows = jnp.dot(order, mixed, preferred_element_type=F32).astype(BF16)
    half = qrows // 2
    qall[d, 0] = sorted_rows[:half]
    qall[d, 1] = sorted_rows[half:]

    def send_y(p):
        return send(qall.at[d, c], qall.at[d, c], y_send.at[p], q_recv.at[d, c], ((y + p) % ny) * nz + z, t)

    lax.fori_loop(1, ny, start_of(send_y), 0)

    far = nz // 2

    def place(j):
        first, last = j < ny, j >= no - ny
        mid = j - ny
        step = jnp.where(first, 0, mid // (2 * ny) + 1)
        r = mid % (2 * ny)
        yy = jnp.where(first, j, jnp.where(last, j - (no - ny), r // 2))
        back = jnp.where(first, 0, jnp.where(last, yy % 2, r % 2))
        zz = (z + nz + jnp.where(back == 0, -step, step)) % nz
        return step, back, yy, yy * nz + zz

    def copies(j):
        step, back, yy, o = place(j)
        own = o == d
        onward = (step < far - 1) | ((step == far - 1) & (yy % 2 == back))
        plus = (step == 0) | ((back == 0) & onward)
        minus = (step == 0) | ((back == 1) & onward)
        block, arrival = qall.at[o, c], q_recv.at[o, c]
        return (
            own, plus, minus, o,
            send(block, block, zp_send.at[j], arrival, y * nz + (z + 1) % nz, t),
            send(block, block, zm_send.at[j], arrival, y * nz + (z + nz - 1) % nz, t),
            send(block, block, sib_send.at[j], arrival, d, sibling),
        )

    def forward(j):
        own, plus, minus, o, to_plus, to_minus, to_sibling = copies(j)

        @pl.when(jnp.logical_not(own))
        def _():
            to_sibling.wait_recv()

        @pl.when(plus)
        def _():
            to_plus.start()

        @pl.when(minus)
        def _():
            to_minus.start()

        @pl.when(jnp.logical_not(own))
        def _():
            to_sibling.start()

    def list_arrived(p, carry):
        src = (d + p) % no
        send(lists_in.at[src], lists_in.at[src], l_send.at[0], l_recv.at[src], src, t).wait_recv()
        return carry

    def forward_body(j, carry):
        forward(j)
        return carry

    ahead = min(AHEAD, no)
    lax.fori_loop(0, ahead, forward_body, 0)
    lax.fori_loop(1, no, list_arrived, 0)
    to_smem = pltpu.make_async_copy(lists_in, lists, s_sem)
    to_smem.start()

    for s in range(no):
        lens_in[s : s + 1] = lists_in[s]
    entry = lens_in[...]
    doc_id = entry & (ndocs - 1)
    lanes = len_ref.shape[1]
    length = jnp.zeros(entry.shape, I32)
    for r in range(len_ref.shape[0]):
        line = jnp.broadcast_to(len_ref[r : r + 1], (no, lanes))
        found = jnp.take_along_axis(line, doc_id % lanes, axis=1)
        length = jnp.where(doc_id // lanes == r, found, length)
    both = jnp.concatenate([entry >> shift, length], axis=0).astype(F32).astype(BF16)
    groups = cap // slots
    width = cap * slots
    lane_row, lane_col = iota((cap, width), 0), iota((cap, width), 1)
    pick = (lane_row == (lane_col % cap) // slots * slots + lane_col // cap).astype(BF16)
    spread = jnp.dot(both, pick, preferred_element_type=F32)
    for s in range(2 * no):
        expand[s] = spread[s : s + 1]

    loads[2].wait()
    to_smem.wait()
    position = (t * slots + iota((8, cap), 1) % slots).astype(F32)
    lane = iota((8, cap), 1)
    per_query = qrows // nq

    def merge(a, b, dist):
        keep = ((lane // dist) % 2 == 0)[None]
        a_back = pltpu.roll(a, cap - dist, 2)
        b_on = pltpu.roll(b, dist, 2)
        return jnp.maximum(jnp.where(keep, a, b_on), jnp.where(keep, a_back, b))

    def compute(j):
        o = place(j)[3]

        @pl.when(o != d)
        def _():
            other = qall.at[o, 1 - c]
            send(other, other, sib_send.at[j], q_recv.at[o, 1 - c], d, sibling).wait_recv()

        query = jnp.concatenate([qall[o, 0], qall[o, 1]], axis=0)

        def tile(v):
            parts = []
            for u in (v, v + slots // 2):
                for g in range(groups):
                    parts.append(docs[lists[o, 0, g * slots + u] & (ndocs - 1)])
            matrix = jnp.concatenate(parts, axis=0)
            sims = lax.dot_general(query, matrix, NT, preferred_element_type=F32)
            out = []
            for h, u in enumerate((v, v + slots // 2)):
                block = sims[:, h * cap : (h + 1) * cap].reshape(nq, per_query // 8, 8, cap)
                whose = jnp.broadcast_to(expand[o, :, u * cap : (u + 1) * cap], (8, cap))
                until = jnp.broadcast_to(expand[o + no, :, u * cap : (u + 1) * cap], (8, cap))
                picked = block[0]
                for q in range(1, nq):
                    picked = jnp.where((whose == q)[None], block[q], picked)
                out.append(jnp.where((position < until)[None], picked, F32(-1e30)))
            return merge(out[0], out[1], slots // 2)

        def tree(v, dist):
            if dist == slots // 2:
                return tile(v)
            return merge(tree(v, dist * 2), tree(v + dist, dist * 2), dist)

        best[j] = tree(0, 1).reshape(per_query, cap)

    def send_best(j):
        return send(best.at[j], inbox.at[j // nt, t], m_send.at[j], m_recv.at[j // nt, t], d, j % nt)

    def send_sum(m, tp):
        o = place(t + nt * m)[3]
        return (o == d) & (tp == t), send(sums.at[m], table.at[d], t_send.at[m, tp], t_recv.at[d], o, tp)

    def reduce(m):
        total = best[t + nt * m]

        def more(p, total):
            src = (t + p) % nt
            send(inbox.at[m, src], inbox.at[m, src], m_send.at[0], m_recv.at[m, src], d, src).wait_recv()
            return jnp.maximum(total, inbox[m, src])

        total = lax.fori_loop(1, nt, more, total)
        sums[m] = jnp.sum(total, axis=0, keepdims=True)

        def give(tp, carry):
            mine, copy = send_sum(m, tp)

            @pl.when(mine)
            def _():
                table[d] = sums[m]

            @pl.when(jnp.logical_not(mine))
            def _():
                copy.start()

            return carry

        lax.fori_loop(0, nt, give, 0)

    def step(j, carry):
        @pl.when(j + ahead < no)
        def _():
            forward(j + ahead)

        compute(j)

        @pl.when(j % nt != t)
        def _():
            send_best(j).start()

        @pl.when((j % nt == nt - 1) & (j >= 2 * nt - 1))
        def _():
            reduce(j // nt - 1)

        return carry

    lax.fori_loop(0, no, step, 0)
    reduce(no // nt - 1)

    def score_arrived(s, carry):
        @pl.when(jnp.logical_not((s == d) & (t == y % nt)))
        def _():
            send(table.at[s], table.at[s], t_send.at[0, 0], t_recv.at[s], s, t).wait_recv()

        return carry

    lax.fori_loop(0, no, score_arrived, 0)

    for s in range(no):
        table2[s : s + 1] = table[s]
    whole = table2[...]
    top = whole.astype(BF16).astype(F32)
    rest = whole - top
    middle = rest.astype(BF16).astype(F32)
    stacked = [top, middle, rest - middle]
    pad = 128 - 3 * no
    stacked.append(jnp.zeros((pad, cap), F32))
    turned = jnp.transpose(jnp.concatenate(stacked, axis=0)).astype(BF16)
    for q in range(nq):
        mine = onehots[q]
        select = jnp.concatenate([mine, mine, mine, jnp.zeros((pad, cands), BF16)], axis=0)
        found = jnp.dot(turned, select, preferred_element_type=F32)
        hit = iota((cap, cands), 0).astype(F32) == ranks[q]
        out_ref[q : q + 1] = jnp.sum(jnp.where(hit, found, F32(0.0)), axis=0, keepdims=True)

    lax.fori_loop(1, nt, sent_of(send_unit), 0)
    lax.fori_loop(1, no, sent_of(send_list), 0)
    lax.fori_loop(1, ny, sent_of(send_y), 0)

    def drained(j, carry):
        own, plus, minus, o, to_plus, to_minus, to_sibling = copies(j)

        @pl.when(plus)
        def _():
            to_plus.wait_send()

        @pl.when(minus)
        def _():
            to_minus.wait_send()

        @pl.when(jnp.logical_not(own))
        def _():
            to_sibling.wait_send()

        @pl.when(j % nt != t)
        def _():
            send_best(j).wait_send()

        return carry

    lax.fori_loop(0, no, drained, 0)

    def sums_left(i, carry):
        mine, copy = send_sum(i // nt, i % nt)

        @pl.when(jnp.logical_not(mine))
        def _():
            copy.wait_send()

        return carry

    lax.fori_loop(0, no, sums_left, 0)


def on_device(ny, nz, nt, query_states, proj_weight, doc_vectors, document_token_length, candidates):
    nq, per, width = query_states.shape
    ndocs, slots, dim = doc_vectors.shape
    cands = candidates.shape[1]
    no = ny * nz
    cap = 2 * nq * cands // no
    rows = nq * per
    dma = pltpu.SemaphoreType.DMA
    vmem, hbm = pl.BlockSpec(memory_space=pltpu.VMEM), pl.BlockSpec(memory_space=pl.ANY)
    return pl.pallas_call(
        functools.partial(kernel, ny, nz, nt),
        out_shape=jax.ShapeDtypeStruct((nq, cands), F32),
        in_specs=[hbm, hbm, hbm, vmem, vmem],
        out_specs=vmem,
        scratch_shapes=[
            pltpu.VMEM((ndocs, slots, dim), BF16),
            pltpu.VMEM((rows, width), BF16),
            pltpu.VMEM((width, dim), BF16),
            pltpu.VMEM((nt, rows, dim), BF16),
            pltpu.VMEM((no, 2, rows * nt // 2, dim), BF16),
            pltpu.VMEM((no, 1, cap), I32),
            pltpu.VMEM((no, 1, cap), I32),
            pltpu.SMEM((no, 1, cap), I32),
            pltpu.VMEM((2 * no, 1, cap * slots), F32),
            pltpu.VMEM((no, cap), I32),
            pltpu.VMEM((nq, no, cands), BF16),
            pltpu.VMEM((nq, 1, cands), F32),
            pltpu.VMEM((no, per * nt, cap), F32),
            pltpu.VMEM((no // nt, nt, per * nt, cap), F32),
            pltpu.VMEM((no // nt, 1, cap), F32),
            pltpu.VMEM((no, 1, cap), F32),
            pltpu.VMEM((no, cap), F32),
            dma((3,)),
            dma((nt,)),
            dma((nt,)),
            dma((no,)),
            dma((no,)),
            dma((no, 2)),
            dma((ny,)),
            dma((no,)),
            dma((no,)),
            dma((no,)),
            dma((no,)),
            dma((no // nt, nt)),
            dma((no // nt, nt)),
            dma((no,)),
            dma,
        ],
        compiler_params=pltpu.CompilerParams(
            collective_id=0, has_side_effects=True, vmem_limit_bytes=48 * 2**20
        ),
    )(
        doc_vectors,
        query_states.reshape(rows, width),
        proj_weight,
        document_token_length.reshape(-1, min(128, ndocs)),
        candidates,
    )


def solution(mesh, ny=4):
    no, nt = mesh.shape["doc"], mesh.shape["tok"]
    placed = (P("doc", "tok", None), P(), P("doc", "tok", None), P("doc"), P("doc", None))
    return jax.shard_map(
        functools.partial(on_device, ny, no // ny, nt),
        mesh=mesh, in_specs=placed, out_specs=P("doc", None), check_vma=False,
    )
```

time: 281 us -> 72.6 us (0.26)
  waiting for transfers between devices: 92.6 us -> 0 us
  local copies, waits for them, and re-layouts: 82 us -> 5.97 us
  Pallas kernels: 0 us -> 66.3 us
  blocking collectives: 33.8 us -> 0 us
  matrix products: 24.4 us -> 0 us
  starting transfers between devices: 19.1 us -> 0 us
  between operations: 13.6 us -> 0.02 us
  other arithmetic: 12.3 us -> 0 us
    pallas_call x0 -> x1, Pallas kernels: none -> 66.3 us  [on_device(): pl.pallas_call(functools.partial(kernel, ny, nz, nt), out_shape=jax.Shape...]
    pmax x1 -> x0, waiting for transfers between devices: 65.3 us -> none  [on_device(): merged = lax.pmax(partial_value, 'tok')]
    gather x17 -> x0, local copies, waits for them, and re-layouts: 58.4 us -> none  [the longest x8 27 us: block_maxima(): document_matrices = doc_vectors[doc_block]]
    dot_general x9 -> x0, matrix products: 24.4 us -> none  [the longest x8 23.3 us: block_maxima(): jnp.einsum('gcki,gri->gckr', document_matrices, query_block, preferred_el...]
    all_to_all x2 -> x0, starting transfers between devices: 19 us -> none  [the longest x1 9.82 us: on_device(): lax.all_to_all(send_query, 'doc', split_axis=0, concat_axis=0, tiled=True)]
    all_gather x1 -> x0, waiting for transfers between devices: 18.7 us -> none  [on_device(): every_query = lax.all_gather(owner_whole, 'doc', axis=0, tiled=True)]
    all_to_all x1 -> x0, blocking collectives: 18 us -> none  [on_device(): lax.all_to_all(slot_scores.reshape(shard_count, capacity), 'doc', split_a...]
    all_gather x1 -> x0, blocking collectives: 15.8 us -> none  [on_device(): owner_whole = lax.all_gather(unit, 'tok', axis=1, tiled=True)]
  transfers between devices with their start and end apart: 4 -> 0, of which waited for: 3 -> 0; matrix products, arithmetic and copies ran while one was open for 10% -> 0% of each run, Pallas kernels for 0% -> 0%
where the time goes in v1:
time: 72.6 us; the launch traced here: 72.3 us
  Pallas kernels  66.3 us (91%)
  local copies, waits for them, and re-layouts  5.97 us (8%)
    pallas_call x1, Pallas kernels, on_device(): pl.pallas_call(functools.partial(kernel, ny, nz, nt), out_shape=jax.Shape...  66.3 us
    unnamed x9, local copies, waits for them, and re-layouts  5.12 us

profile of v1, /device:TPU:1, one launch (start us, length us, event | category | flops | bytes accessed | tf_op | source)
XLA Modules:
  0.0 72.3 jit_solution(11935436622240681769)
XLA Ops:
  0.0 0.9 %reshape.6.qs_hbm = bf16[32,1024]{1,0:T(8,128)(2,1)S(1)} reshape(bf16[8,4,1024]{2,1,0:T(4,128)(2,1)} %param.5) | data formatting | bytes 131072 | tf_op jit(solution)/shard_map/reshape | solution.py:442
  0.9 0.0 copy-start
  0.9 2.2 %copy-done = bf16[1024,16,128]{2,1,0:T(8,128)(2,1)S(1)} copy-done((bf16[1024,16,128]{2,1,0:T(8,128)(2,1)S(1)}, bf16[1024,16,128]{2,1,0:T(8,128)(2,1)}, u32[]{:S(2)}) %copy-start) | copy-done | bytes 4194328
  3.1 0.0 copy-start.1
  3.1 0.9 %copy-done.1 = bf16[1024,128]{1,0:T(8,128)(2,1)S(1)} copy-done((bf16[1024,128]{1,0:T(8,128)(2,1)S(1)}, bf16[1024,128]{1,0:T(8,128)(2,1)}, u32[]{:S(2)}) %copy-start.1) | copy-done | bytes 262168
  4.0 0.0 copy-start.2
  4.0 0.7 copy-done.2
  4.7 0.0 copy-start.3
  4.7 0.7 copy-done.3
  5.4 66.3 %shard_map.55 = f32[8,256]{1,0:T(8,128)S(1)} custom-call(bf16[1024,16,128]{2,1,0:T(8,128)(2,1)S(1)} %copy-done, bf16[32,1024]{1,0:T(8,128)(2,1)S(1)} %reshape.6.qs_hbm, bf16[1024,128]{1,0:T(8,128)(2,1)S(1)} %copy-done.1, s32[8,128]{1,0:T(8,128)S(1)} %bitcast.1, s32[8,256]{1,0:T(8,128)S(1)} %copy-done.2), custom_call_target="tpu_custom_call" | custom-call | tf_op jit(solution)/shard_map/pallas_call | solution.py:398
  71.7 0.6 copy.7
Async XLA Ops:
  0.9 2.2 %copy-start = (bf16[1024,16,128]{2,1,0:T(8,128)(2,1)S(1)}, bf16[1024,16,128]{2,1,0:T(8,128)(2,1)}, u32[]{:S(2)}) copy-start(bf16[1024,16,128]{2,1,0:T(8,128)(2,1)} %docs_hbm.1) | copy-start | bytes 12582916
  3.1 0.9 %copy-start.1 = (bf16[1024,128]{1,0:T(8,128)(2,1)S(1)}, bf16[1024,128]{1,0:T(8,128)(2,1)}, u32[]{:S(2)}) copy-start(bf16[1024,128]{1,0:T(8,128)(2,1)} %w_hbm.1) | copy-start | bytes 786436
  4.0 0.7 copy-start.2
  4.7 0.7 copy-start.3

commit v2 on v1

v2 whole, which is shorter than its diff:
```python
import functools

import jax
import jax.numpy as jnp
from jax import lax
from jax.experimental import pallas as pl
from jax.experimental.pallas import tpu as pltpu
from jax.sharding import PartitionSpec as P

MESH = pl.DeviceIdType.MESH
F32, BF16, I32 = jnp.float32, jnp.bfloat16, jnp.int32
NT = (((1,), (1,)), ((), ()))
GROUP = 4
WAVES = ((3, 4), (5, 6), (), (7,))
LAG = 4


def iota(shape, dim):
    return lax.broadcasted_iota(I32, shape, dim)


def schedule(ny, nz):
    half = nz // 2
    steps = [0.0] + [1.9 + 1.1 * ((k + 1) // 2) for k in range(1, nz)]
    steps[nz - 1] += 1.0 if half > 2 else 0.0
    entries = [(steps[k] + (3.4 if p else 0.0), p, k) for k in range(nz) for p in range(ny)]
    return [(k, p) for _, p, k in sorted(entries, key=lambda e: (e[0], e[2], e[1]))]


def kernel(
    ny, nz, nt, docs_hbm, qs_hbm, w_hbm, len_hbm, cand_hbm, out_ref,
    docs, qs, qrow, w, len_ref, cand_ref, ublk, qall, lists_out, lists_z, lists_in, lists, combs, onehots, ranks,
    raw, best, inbox, sums, table, table2,
    in_sem, a_send, a_recv, z_send, y_send, sib_send, q_recv, l_send, l_recv, yl_send, yl_recv,
    m_send, m_recv, t_send, t_recv, s_sem,
):
    no = ny * nz
    d, t = lax.axis_index("doc"), lax.axis_index("tok")
    y, z, c = d // nz, d % nz, t % 2
    sibling = t + 1 - 2 * c
    nq, cands = cand_ref.shape
    ndocs = docs.shape[0]
    slots = docs.shape[1]
    shift = ndocs.bit_length() - 1
    per = qs.shape[1]
    qrows = nq * per * nt
    per_query = per * nt
    cap = lists_in.shape[2]
    order = schedule(ny, nz)
    groups = no // GROUP

    pairs = ((qs_hbm, qs), (w_hbm, w), (cand_hbm, cand_ref), (len_hbm, len_ref), (docs_hbm, docs))
    loads = [pltpu.make_async_copy(src, dst, in_sem.at[i]) for i, (src, dst) in enumerate(pairs)]
    for load in loads:
        load.start()

    barrier = pltpu.get_barrier_semaphore()

    def greet(doc, tok):
        pl.semaphore_signal(barrier, inc=1, device_id={"doc": doc, "tok": tok}, device_id_type=MESH)

    for p in range(1, nz):
        greet(y * nz + (z + p) % nz, t)
    for p in range(1, ny):
        greet(((y + p) % ny) * nz + z, t)
    for p in range(1, nt):
        greet(d, (t + p) % nt)

    def send(src, dst, ssem, rsem, doc, tok):
        return pltpu.make_async_remote_copy(
            src_ref=src, dst_ref=dst, send_sem=ssem, recv_sem=rsem,
            device_id={"doc": doc, "tok": tok}, device_id_type=MESH,
        )

    def loop(first, last, do):
        def body(i, carry):
            do(i)
            return carry

        lax.fori_loop(first, last, body, 0)

    loads[0].wait()
    for q in range(nq):
        qrow[per * q : per * (q + 1)] = qs[q].astype(F32)
    loads[1].wait()
    proj = jnp.dot(qrow[...].astype(BF16), w[...], preferred_element_type=F32)
    unit = proj * lax.rsqrt(jnp.sum(proj * proj, axis=-1, keepdims=True) + 1e-06)
    ublk[t] = unit.astype(BF16)

    pl.semaphore_wait(barrier, nt - 1 + nz - 1 + ny - 1)

    def send_unit(p):
        return send(ublk.at[t], ublk.at[t], a_send.at[p], a_recv.at[t], d, (t + p) % nt)

    for p in range(1, nt):
        send_unit(p).start()

    loads[2].wait()
    cand = cand_ref[...]
    shard_rows = []
    for q in range(nq):
        shard_rows.append((iota((no, cands), 0) == (cand[q : q + 1] >> shift)).astype(F32))
    before = (iota((cands, cands), 0) < iota((cands, cands), 1)).astype(BF16)
    prefix = jnp.dot(
        jnp.concatenate(shard_rows, axis=0).astype(BF16), before, preferred_element_type=F32
    )
    base = jnp.zeros((no, 1), F32)
    coded = jnp.zeros((2 * no, cap), F32)
    for q in range(nq):
        mine = shard_rows[q]
        rank = jnp.sum(mine * (prefix[no * q : no * (q + 1)] + base), axis=0, keepdims=True)
        base = base + jnp.sum(mine, axis=1, keepdims=True)
        ranks[q] = rank
        onehots[q] = mine.astype(BF16)
        local = cand[q : q + 1] & (ndocs - 1)
        high = (local >> 8) + (ndocs >> 8) * q
        low = local & 255
        rank_rows = (iota((cap, cands), 0).astype(F32) == rank).astype(BF16)
        lhs = jnp.concatenate([mine * high.astype(F32), mine * low.astype(F32)], axis=0)
        coded = coded + lax.dot_general(lhs.astype(BF16), rank_rows, NT, preferred_element_type=F32)
    packed = coded[:no].astype(I32) * 256 + coded[no:].astype(I32)
    for s in range(no):
        lists_out[s % nz, s // nz] = packed[s : s + 1]
    lists_z[z] = lists_out[z]

    def offset(k):
        return jnp.where(k % 2 == 1, (k + 1) // 2, -(k // 2))

    def send_list(k):
        to = (z + nz + offset(k)) % nz
        return send(lists_out.at[to], lists_z.at[z], l_send.at[k], l_recv.at[z], y * nz + to, t)

    loop(1, nz, lambda k: send_list(k).start())

    row, col = iota((qrows, qrows), 0), iota((qrows, qrows), 1)
    from_row = ((row // per) % nt) * (per * nq) + (row // per_query) * per + row % per
    sorting = (from_row == col).astype(BF16)

    def unit_arrived(p):
        src = (t + p) % nt
        send(ublk.at[src], ublk.at[src], a_send.at[0], a_recv.at[src], d, src).wait_recv()

    loop(1, nt, unit_arrived)
    mixed = jnp.concatenate([ublk[i] for i in range(nt)], axis=0)
    sorted_rows = jnp.dot(sorting, mixed, preferred_element_type=F32).astype(BF16)
    half = qrows // 2
    qall[d, 0] = sorted_rows[:half]
    qall[d, 1] = sorted_rows[half:]

    def send_z(k):
        to = (z + nz + offset(k)) % nz
        return send(qall.at[d, c], qall.at[d, c], z_send.at[k], q_recv.at[d, c], y * nz + to, t)

    loop(1, nz, lambda k: send_z(k).start())

    def owner(k, p):
        return ((y + p) % ny) * nz + (z + nz + offset(k)) % nz

    def send_y(k, p):
        o = owner(k, 0)
        return send(qall.at[o, c], qall.at[o, c], y_send.at[k, p], q_recv.at[o, c], ((y + p) % ny) * nz + z, t)

    def send_row(k, p):
        o, to = owner(k, 0), (y + p) % ny
        return send(lists_z.at[o % nz, to], lists_in.at[o], yl_send.at[k, p], yl_recv.at[o], to * nz + z, t)

    def share(o):
        return send(qall.at[o, c], qall.at[o, c], sib_send.at[o], q_recv.at[o, c], d, sibling)

    def forward(k, own=False):
        o = owner(k, 0)
        if not own:
            share(o).wait_recv()
        for p in range(1, ny):
            send_y(k, p).start()
        if not own:
            share(o).start()
            send(lists_z.at[o % nz], lists_z.at[o % nz], l_send.at[0], l_recv.at[o % nz], o, t).wait_recv()
        for p in range(1, ny):
            send_row(k, p).start()
        lists_in[o] = lists_z[o % nz, y]

    def to_smem(o):
        return pltpu.make_async_copy(lists_in.at[o], lists.at[o], s_sem.at[o])

    def entry(g, i):
        k, p = jnp.int32(0), jnp.int32(0)
        for n in range(groups):
            k = jnp.where(g == n, order[GROUP * n + i][0], k)
            p = jnp.where(g == n, order[GROUP * n + i][1], p)
        return k, p, owner(k, p)

    def receive(g):
        for i in range(GROUP):
            k, p, o = entry(g, i)

            @pl.when(p != 0)
            def _():
                share(o).wait_recv()
                share(o).start()
                send(lists_in.at[o], lists_in.at[o], l_send.at[0], yl_recv.at[o], o, t).wait_recv()

            to_smem(o).start()

    def complete(g):
        for i in range(GROUP):
            k, p, o = entry(g, i)

            @pl.when(o != d)
            def _():
                other = qall.at[o, 1 - c]
                send(other, other, sib_send.at[o], q_recv.at[o, 1 - c], d, sibling).wait_recv()

            to_smem(o).wait()

    lane = iota((8, cap), 1)
    lanes = len_ref.shape[1]
    position = t * slots + lane % slots
    blocks = cap // slots

    def combine(o):
        line = jnp.broadcast_to(lists_in[o], (8, cap))
        doc_id = line & (ndocs - 1)
        length = jnp.zeros((8, cap), I32)
        for r in range(len_ref.shape[0]):
            found = jnp.take_along_axis(
                jnp.broadcast_to(len_ref[r : r + 1], (8, lanes)), doc_id % lanes, axis=1
            )
            length = jnp.where(doc_id // lanes == r, found, length)
        combs[o] = (line >> shift) * 256 + length

    def merge(a, b, dist):
        keep = ((lane // dist) % 2 == 0)[None]
        a_back = pltpu.roll(a, cap - dist, 2)
        b_on = pltpu.roll(b, dist, 2)
        return jnp.maximum(jnp.where(keep, a, b_on), jnp.where(keep, a_back, b))

    def tile(o, query, comb, v):
        both = (v, v + slots // 2)
        parts = []
        for u in both:
            for n in range(blocks):
                parts.append(docs[lists[o, 0, n * slots + u] & (ndocs - 1)])
        sims = lax.dot_general(query, jnp.concatenate(parts, axis=0), NT, preferred_element_type=F32)
        out = []
        for h, u in enumerate(both):
            block = sims[:, h * cap : (h + 1) * cap].reshape(nq, per_query // 8, 8, cap)
            here = jnp.take_along_axis(comb, (lane // slots) * slots + u, axis=1)
            whose, until = here >> 8, here & 255
            picked = block[0]
            for q in range(1, nq):
                picked = jnp.where((whose == q)[None], block[q], picked)
            out.append(jnp.where((position < until)[None], picked, F32(-1e30)))
        return out

    def fold(leaf, v, dist):
        if dist == slots // 2:
            return merge(*leaf(v), dist)
        return merge(fold(leaf, v, dist * 2), fold(leaf, v + dist, dist * 2), dist)

    def put(j, value):
        best[j + 1] = value.reshape(per_query, cap)

    def kept(v):
        return raw[v], raw[v + slots // 2]

    def compute(g):
        put(GROUP * g - 1, fold(kept, 0, 1))
        for i in range(GROUP):
            o = entry(g, i)[2]
            query = jnp.concatenate([qall[o, 0], qall[o, 1]], axis=0)
            comb = combs[o]
            leaf = functools.partial(tile, o, query, comb)
            if i < GROUP - 1:
                put(GROUP * g + i, fold(leaf, 0, 1))
            else:
                for v in range(slots // 2):
                    raw[v], raw[v + slots // 2] = leaf(v)
        for i in range(GROUP):
            combine(entry(jnp.minimum(g + 1, groups - 1), i)[2])

    def send_best(j):
        return send(best.at[j + 1], inbox.at[j // nt, t], m_send.at[j], m_recv.at[j // nt, t], d, j % nt)

    def give_best(j):
        @pl.when((j >= 0) & (j % nt != t))
        def _():
            send_best(j).start()

    def target(m):
        j = t + nt * m
        o = jnp.int32(0)
        for i in range(GROUP):
            o = jnp.where(j % GROUP == i, entry(j // GROUP, i)[2], o)
        return o

    def send_sum(m, tp, o):
        return (o == d) & (tp == t), send(sums.at[m], table.at[d], t_send.at[m, tp], t_recv.at[d], o, tp)

    def reduce(m):
        total = best[t + nt * m + 1]

        def more(p, total):
            src = (t + p) % nt
            send(inbox.at[m, src], inbox.at[m, src], m_send.at[0], m_recv.at[m, src], d, src).wait_recv()
            return jnp.maximum(total, inbox[m, src])

        total = lax.fori_loop(1, nt, more, total)
        sums[m] = jnp.sum(total, axis=0, keepdims=True)
        o = target(m)

        def give(tp):
            mine, copy = send_sum(m, tp, o)

            @pl.when(mine)
            def _():
                table[d] = sums[m]

            @pl.when(jnp.logical_not(mine))
            def _():
                copy.start()

        loop(0, nt, give)

    forward(0, own=True)
    loop(1, min(3, nz), forward)
    receive(0)
    loads[3].wait()
    for i in range(GROUP):
        combine(entry(0, i)[2])
    loads[4].wait()

    passing = {n: [k for k in WAVES[n] if k < nz] for n in range(min(groups, len(WAVES)))}
    summing = [(nt * (m + 1) - 1) // GROUP + LAG for m in range(no // nt)]

    def step(g):
        for n, ks in passing.items():
            if ks:

                @pl.when(g == n)
                def _():
                    loop(ks[0], ks[-1] + 1, forward)

        @pl.when(g < groups - 1)
        def _():
            receive(g + 1)

        complete(g)
        compute(g)
        for i in range(GROUP):
            give_best(GROUP * g + i - 1)
        for m, n in enumerate(summing):
            if n < groups:
                pl.when(g == n)(functools.partial(reduce, m))

    loop(0, groups, step)
    put(no - 1, fold(kept, 0, 1))
    give_best(jnp.int32(no - 1))
    for m, n in enumerate(summing):
        if n >= groups:
            reduce(m)

    def drained_units(p):
        send_unit(p).wait_send()

    def drained_z(k):
        send_z(k).wait_send()
        send_list(k).wait_send()

    def drained_y(k):
        for p in range(1, ny):
            send_y(k, p).wait_send()
            send_row(k, p).wait_send()

    def drained_owner(o):
        @pl.when(o != d)
        def _():
            share(o).wait_send()

        @pl.when(o % nt != t)
        def _():
            send_best(o).wait_send()

    loop(1, nt, drained_units)
    loop(1, nz, drained_z)
    loop(0, nz, drained_y)
    loop(0, no, drained_owner)

    def score_arrived(s):
        @pl.when(jnp.logical_not((s == d) & (t == order.index((0, 0)) % nt)))
        def _():
            send(table.at[s], table.at[s], t_send.at[0, 0], t_recv.at[s], s, t).wait_recv()

    loop(0, no, score_arrived)

    for s in range(no):
        table2[s : s + 1] = table[s]
    whole = table2[...]
    top = whole.astype(BF16).astype(F32)
    rest = whole - top
    middle = rest.astype(BF16).astype(F32)
    stacked = [top, middle, rest - middle]
    pad = 128 - 3 * no
    stacked.append(jnp.zeros((pad, cap), F32))
    turned = jnp.transpose(jnp.concatenate(stacked, axis=0)).astype(BF16)
    for q in range(nq):
        mine = onehots[q]
        select = jnp.concatenate([mine, mine, mine, jnp.zeros((pad, cands), BF16)], axis=0)
        found = jnp.dot(turned, select, preferred_element_type=F32)
        hit = iota((cap, cands), 0).astype(F32) == ranks[q]
        out_ref[q : q + 1] = jnp.sum(jnp.where(hit, found, F32(0.0)), axis=0, keepdims=True)

    def sums_left(i):
        mine, copy = send_sum(i // nt, i % nt, target(i // nt))

        @pl.when(jnp.logical_not(mine))
        def _():
            copy.wait_send()

    loop(0, no, sums_left)


def on_device(ny, nz, nt, query_states, proj_weight, doc_vectors, document_token_length, candidates):
    nq, per, width = query_states.shape
    ndocs, slots, dim = doc_vectors.shape
    cands = candidates.shape[1]
    no = ny * nz
    cap = 2 * nq * cands // no
    rows = nq * per
    lanes = min(128, ndocs)
    dma = pltpu.SemaphoreType.DMA
    hbm = pl.BlockSpec(memory_space=pl.ANY)
    return pl.pallas_call(
        functools.partial(kernel, ny, nz, nt),
        out_shape=jax.ShapeDtypeStruct((nq, cands), F32),
        in_specs=[hbm] * 5,
        out_specs=pl.BlockSpec(memory_space=pltpu.VMEM),
        scratch_shapes=[
            pltpu.VMEM((ndocs, slots, dim), BF16),
            pltpu.VMEM((nq, per, width), BF16),
            pltpu.VMEM((rows, width), F32),
            pltpu.VMEM((width, dim), BF16),
            pltpu.VMEM((ndocs // lanes, lanes), I32),
            pltpu.VMEM((nq, cands), I32),
            pltpu.VMEM((nt, rows, dim), BF16),
            pltpu.VMEM((no, 2, rows * nt // 2, dim), BF16),
            pltpu.VMEM((nz, ny, 1, cap), I32),
            pltpu.VMEM((nz, ny, 1, cap), I32),
            pltpu.VMEM((no, 1, cap), I32),
            pltpu.SMEM((no, 1, cap), I32),
            pltpu.VMEM((no, 8, cap), I32),
            pltpu.VMEM((nq, no, cands), BF16),
            pltpu.VMEM((nq, 1, cands), F32),
            pltpu.VMEM((slots, per * nt // 8, 8, cap), F32),
            pltpu.VMEM((no + 1, per * nt, cap), F32),
            pltpu.VMEM((no // nt, nt, per * nt, cap), F32),
            pltpu.VMEM((no // nt, 1, cap), F32),
            pltpu.VMEM((no, 1, cap), F32),
            pltpu.VMEM((no, cap), F32),
            dma((5,)),
            dma((nt,)),
            dma((nt,)),
            dma((nz,)),
            dma((nz, ny)),
            dma((no,)),
            dma((no, 2)),
            dma((nz,)),
            dma((nz,)),
            dma((nz, ny)),
            dma((no,)),
            dma((no,)),
            dma((no // nt, nt)),
            dma((no // nt, nt)),
            dma((no,)),
            dma((no,)),
        ],
        compiler_params=pltpu.CompilerParams(
            collective_id=0, has_side_effects=True, vmem_limit_bytes=60 * 2**20
        ),
    )(
        doc_vectors,
        query_states,
        proj_weight,
        document_token_length.reshape(-1, lanes),
        candidates,
    )


def solution(mesh, ny=4):
    no, nt = mesh.shape["doc"], mesh.shape["tok"]
    placed = (P("doc", "tok", None), P(), P("doc", "tok", None), P("doc"), P("doc", None))
    return jax.shard_map(
        functools.partial(on_device, ny, no // ny, nt),
        mesh=mesh, in_specs=placed, out_specs=P("doc", None), check_vma=False,
    )
```

time: 72.6 us -> 54.4 us (0.75)
  Pallas kernels: 66.3 us -> 52.9 us
  local copies, waits for them, and re-layouts: 5.97 us -> 1.3 us
    pallas_call x1, Pallas kernels: 66.3 us -> 52.9 us  [on_device(): pl.pallas_call(functools.partial(kernel, ny, nz, nt), out_shape=jax.Shape...]
    unnamed x9 -> x1, local copies, waits for them, and re-layouts: 5.12 us -> 1.3 us
    reshape x1 -> x0, local copies, waits for them, and re-layouts: 0.86 us -> none  [on_device(): query_states.reshape(rows, width)]
where the time goes in v2:
time: 54.4 us; the launch traced here: 54.3 us
  Pallas kernels  52.9 us (97%)
  local copies, waits for them, and re-layouts  1.3 us (2%)
    pallas_call x1, Pallas kernels, on_device(): pl.pallas_call(functools.partial(kernel, ny, nz, nt), out_shape=jax.Shape...  52.9 us
    unnamed x1, local copies, waits for them, and re-layouts  1.3 us

profile of v2, /device:TPU:1, one launch (start us, length us, event | category | flops | bytes accessed | tf_op | source)
XLA Modules:
  0.0 54.3 jit_solution(6266985576038622700)
XLA Ops:
  0.0 52.9 %shard_map.55 = f32[8,256]{1,0:T(8,128)} custom-call(bf16[1024,16,128]{2,1,0:T(8,128)(2,1)} %docs_hbm.1, bf16[8,4,1024]{2,1,0:T(4,128)(2,1)} %qs_hbm.1, bf16[1024,128]{1,0:T(8,128)(2,1)} %w_hbm.1, s32[8,128]{1,0:T(8,128)} %bitcast.1, s32[8,256]{1,0:T(8,128)} %cand_hbm.1), custom_call_target="tpu_custom_call" | custom-call | tf_op jit(solution)/shard_map/pallas_call | solution.py:433
  53.0 1.3 %copy.7 = f32[8,256]{1,0:T(8,128)} copy(f32[8,256]{1,0:T(8,128)} %shard_map.55) | data formatting | bytes 16384

commit v3 on v2

v3 whole, which is shorter than its diff:
```python
import functools

import jax
import jax.numpy as jnp
from jax import lax
from jax.experimental import pallas as pl
from jax.experimental.pallas import tpu as pltpu
from jax.sharding import PartitionSpec as P

MESH = pl.DeviceIdType.MESH
F32, BF16, I32 = jnp.float32, jnp.bfloat16, jnp.int32
NT = (((1,), (1,)), ((), ()))
GROUP = 2
LAG = 4


def iota(shape, dim):
    return lax.broadcasted_iota(I32, shape, dim)


def along(k):
    return (k + 1) // 2 if k % 2 else -(k // 2)


def schedule(ny, nz):
    near = [5.0 + 1.0 * m for m in range(nz // 2)]
    entries = [(near[m] + (3.0 if p else 0.0), m, p) for m in range(nz // 2) for p in range(ny)]
    return [(m, p) for _, m, p in sorted(entries)]


def kernel(
    ny, nz, nt, docs_hbm, qs_hbm, w_hbm, len_hbm, cand_hbm, out_ref,
    docs, docs2, qs, qrow, w, len_ref, cand_ref, ublk, pieces, qall, sorting, lists_out, lists_z, lists_in, lists, combs, onehots, ranks,
    sorted_q, raw, best, inbox, sums, table, table2,
    in_sem, a_send, a_recv, b_send, b_recv, v_send, v_recv, z_send, z_recv, y_send, d_send, d_recv, q_recv, l_send, l_recv, yl_send, yl_recv,
    m_send, m_recv, t_send, t_recv, s_sem,
):
    no = ny * nz
    d, t = lax.axis_index("doc"), lax.axis_index("tok")
    y, z, c = d // nz, d % nz, t % 2
    sibling = t + 1 - 2 * c
    nq, cands = cand_ref.shape
    ndocs = docs.shape[0]
    slots = docs.shape[1]
    shift = ndocs.bit_length() - 1
    per = qs.shape[1]
    qrows = nq * per * nt
    per_query = per * nt
    cap = lists_in.shape[2]
    order = schedule(ny, nz)
    groups = no // 2 // GROUP
    nx = nt // 2
    x, odd = t // 2, (z + c) % 2
    places = [[k for k in range(nz) if along(k) % 2 == side] for side in (0, 1)]

    pairs = ((qs_hbm, qs), (w_hbm, w), (cand_hbm, cand_ref), (len_hbm, len_ref), (docs_hbm, docs))
    loads = [pltpu.make_async_copy(src, dst, in_sem.at[i]) for i, (src, dst) in enumerate(pairs)]
    for load in loads:
        load.start()

    barrier = pltpu.get_barrier_semaphore()

    def greet(doc, tok):
        pl.semaphore_signal(barrier, inc=1, device_id={"doc": doc, "tok": tok}, device_id_type=MESH)

    for p in range(1, nz):
        greet(y * nz + (z + p) % nz, t)
    for p in range(1, ny):
        greet(((y + p) % ny) * nz + z, t)
    for p in range(1, nt):
        greet(d, (t + p) % nt)

    def send(src, dst, ssem, rsem, doc, tok):
        return pltpu.make_async_remote_copy(
            src_ref=src, dst_ref=dst, send_sem=ssem, recv_sem=rsem,
            device_id={"doc": doc, "tok": tok}, device_id_type=MESH,
        )

    def loop(first, last, do):
        def body(i, carry):
            do(i)
            return carry

        lax.fori_loop(first, last, body, 0)

    loads[0].wait()
    for q in range(nq):
        qrow[per * q : per * (q + 1)] = qs[q].astype(F32)
    loads[1].wait()
    proj = jnp.dot(qrow[...].astype(BF16), w[...], preferred_element_type=F32)
    unit = proj * lax.rsqrt(jnp.sum(proj * proj, axis=-1, keepdims=True) + 1e-06)
    ublk[0] = unit.astype(BF16)

    pl.semaphore_wait(barrier, nt - 1 + nz - 1 + ny - 1)

    def offset(k):
        return jnp.where(k % 2 == 1, (k + 1) // 2, -(k // 2))

    def send_z(k):
        to = (z + nz - offset(k)) % nz
        return send(ublk.at[0], ublk.at[k], z_send.at[k], z_recv.at[k], y * nz + to, t)

    def core_of(k):
        return (z + along(k) % 2) % 2

    def rank_of(k):
        return places[along(k) % 2].index(k)

    def to_core(k, p):
        return (x + p) % nx * 2 + core_of(k)

    def send_tok(k, p):
        return send(ublk.at[k], qall.at[rank_of(k), 0, t], a_send.at[k, p], a_recv.at[k, t], d, to_core(k, p))

    def rest(k):
        return qall.at[rank_of(k), pl.ds(1, ny - 1), t]

    def send_rest(k, p):
        return send(
            pieces.at[rank_of(k), pl.ds(1, ny - 1)], rest(k), b_send.at[k, p], b_recv.at[k, t], d, to_core(k, p)
        )

    def send_piece(k, p):
        return send(
            ublk.at[k], pieces.at[rank_of(k), ny - p], v_send.at[k, p], v_recv.at[k, ny - p],
            ((y + p) % ny) * nz + z, t,
        )

    def each_tok(k, make, do):
        pl.when(core_of(k) != c)(lambda: do(make(k, 0)))
        for p in range(1, nx):
            do(make(k, p))

    def go(copy):
        copy.start()

    def left(copy):
        copy.wait_send()

    for k in range(1, nz):
        send_z(k).start()
    def spread(k):
        each_tok(k, send_tok, go)
        if along(k) % 2:
            for p in range(1, ny):
                send_piece(k, p).start()

        @pl.when(core_of(k) == c)
        def _():
            qall[rank_of(k), 0, t] = ublk[k]

    spread(0)

    loads[2].wait()
    cand = cand_ref[...]
    shard_rows = []
    for q in range(nq):
        shard_rows.append((iota((no, cands), 0) == (cand[q : q + 1] >> shift)).astype(F32))
    before = (iota((cands, cands), 0) < iota((cands, cands), 1)).astype(BF16)
    prefix = jnp.dot(
        jnp.concatenate(shard_rows, axis=0).astype(BF16), before, preferred_element_type=F32
    )
    base = jnp.zeros((no, 1), F32)
    coded = jnp.zeros((2 * no, cap), F32)
    for q in range(nq):
        mine = shard_rows[q]
        rank = jnp.sum(mine * (prefix[no * q : no * (q + 1)] + base), axis=0, keepdims=True)
        base = base + jnp.sum(mine, axis=1, keepdims=True)
        number = rank.astype(I32)
        ranks[q] = (number % (cap // slots)) * slots + number // (cap // slots)
        onehots[q] = mine.astype(BF16)
        local = cand[q : q + 1] & (ndocs - 1)
        high = (local >> 8) + (ndocs >> 8) * q
        low = local & 255
        rank_rows = (iota((cap, cands), 0).astype(F32) == rank).astype(BF16)
        lhs = jnp.concatenate([mine * high.astype(F32), mine * low.astype(F32)], axis=0)
        coded = coded + lax.dot_general(lhs.astype(BF16), rank_rows, NT, preferred_element_type=F32)
    packed = coded[:no].astype(I32) * 256 + coded[no:].astype(I32)
    packed = jnp.where(iota((no, cap), 1).astype(F32) < base, packed, (nq - 1) * ndocs)
    for s in range(no):
        lists_out[s % nz, s // nz] = packed[s : s + 1]
    lists_z[z] = lists_out[z]

    def send_list(k):
        to = (z + nz + offset(k)) % nz
        return send(lists_out.at[to], lists_z.at[z], l_send.at[k], l_recv.at[z], y * nz + to, t)

    pl.when(c == z % 2)(lambda: loop(1, nz, lambda k: send_list(k).start()))

    row, col = iota((qrows, qrows), 0), iota((qrows, qrows), 1)
    from_row = ((row // per) % nt) * (per * nq) + (row // per_query) * per + row % per
    sorting[...] = (from_row == col).astype(BF16)

    def relay(k):
        send_z(k).wait_recv()
        spread(k)

    def relay_rest(k):
        for p in range(1, ny):
            send_piece(k, ny - p).wait_recv()
        each_tok(k, send_rest, go)

        @pl.when(core_of(k) == c)
        def _():
            for p in range(1, ny):
                qall[rank_of(k), p, t] = pieces[rank_of(k), p]

    def owner(k, p):
        return ((y + p) % ny) * nz + (z + nz + offset(k)) % nz

    def send_y(m, p):
        return send(
            qall.at[m, 0], qall.at[m, ny - p], y_send.at[m, p], q_recv.at[m, ny - p], ((y + p) % ny) * nz + z, t
        )

    def send_row(m, p):
        o, to = owner(place(m), 0), (y + p) % ny
        slot = m * ny + ny - p
        return send(
            lists_z.at[o % nz, to], lists_in.at[slot], yl_send.at[m, p], yl_recv.at[slot], to * nz + z, t
        )

    def place(m):
        return jnp.where(odd == 0, places[0][m], places[1][m])

    def gathered(k, arrivals):
        for p in range(1, nt):
            src = (t + p) % nt
            send(ublk.at[0], ublk.at[0], d_send, arrivals.at[k, src], d, sibling).wait_recv()

    def gathered_rest(k):
        for p in range(1, nt):
            src = (t + p) % nt
            part = pieces.at[0, pl.ds(1, ny - 1)]
            send(part, part, d_send, b_recv.at[k, src], d, sibling).wait_recv()

    def forward(m):
        @pl.when(odd == 0)
        def _():
            gathered(places[0][m], a_recv)
            for p in range(1, ny):
                send_y(m, p).start()

    def forward_list(m):
        k = place(m)
        o = owner(k, 0)

        @pl.when(k != 0)
        def _():
            send(lists_z.at[o % nz], lists_z.at[o % nz], l_send.at[0], l_recv.at[o % nz], d, sibling).wait_recv()

        for p in range(1, ny):
            send_row(m, p).start()
        lists_in[m * ny] = lists_z[o % nz, y]

    def row_arrived(m, p):
        slot = m * ny + p
        send(lists_in.at[slot], lists_in.at[slot], d_send, yl_recv.at[slot], d, sibling).wait_recv()

    def entry(g, i):
        m, k, p = jnp.int32(0), jnp.int32(0), jnp.int32(0)
        for n in range(groups):
            step_m, step_p = order[GROUP * n + i]
            m = jnp.where(g == n, step_m, m)
            k = jnp.where(g == n, place(step_m), k)
            p = jnp.where(g == n, step_p, p)
        return m, k, p, owner(k, p), m * ny + p

    def complete(g):
        for i in range(GROUP):
            m, k, p, _, _ = entry(g, i)

            @pl.when((odd == 0) & (p != 0))
            def _():
                send(qall.at[m, p], qall.at[m, p], d_send, q_recv.at[m, p], d, sibling).wait_recv()

            @pl.when((odd == 1) & (p == 0))
            def _():
                gathered(k, a_recv)

            @pl.when((odd == 1) & (p == 1))
            def _():
                gathered_rest(k)

    lane = iota((8, cap), 1)
    lanes = len_ref.shape[1]
    position = t * slots + lane % slots
    position2 = sibling * slots + lane % slots
    blocks = cap // slots

    def combine(slot):
        line = jnp.broadcast_to(lists_in[slot], (8, cap))
        doc_id = line & (ndocs - 1)
        length = jnp.zeros((8, cap), I32)
        for r in range(len_ref.shape[0]):
            found = jnp.take_along_axis(
                jnp.broadcast_to(len_ref[r : r + 1], (8, lanes)), doc_id % lanes, axis=1
            )
            length = jnp.where(doc_id // lanes == r, found, length)
        combs[slot] = (line >> shift) * 256 + length

    def merge(a, b, dist):
        keep = ((lane // dist) % 2 == 0)[None]
        a_back = pltpu.roll(a, cap - dist, 2)
        b_on = pltpu.roll(b, dist, 2)
        return jnp.maximum(jnp.where(keep, a, b_on), jnp.where(keep, a_back, b))

    window = nq // 2

    def starts(o):
        first, extra = [], jnp.int32(0)
        for v in range(blocks):
            first.append(jnp.minimum((lists[o, 0, slots * v] >> shift) & (nq - 1), nq - window))
            last = (lists[o, 0, slots * v + slots - 1] >> shift) & (nq - 1)
            extra = extra + jnp.where(last - first[v] >= window, v, 0)
        return first, extra & (blocks - 1)

    def product(o, query, v):
        picks = [lists[o, 0, slots * v + n] & (ndocs - 1) for n in range(slots)]
        out = []
        for source in (docs, docs2):
            matrix = jnp.concatenate([source[i] for i in picks], axis=0)
            out.append(lax.dot_general(query, matrix, NT, preferred_element_type=F32))
        return out

    def chosen(sims, h, whose, start, picked):
        block = sims[:, h * cap : (h + 1) * cap].reshape(window, per_query // 8, 8, cap)
        for q in range(window):
            here = block[q] if picked is None else jnp.where((whose == start + q)[None], block[q], picked)
            picked = here
        return picked

    def spread_comb(comb, v, h):
        return jnp.take_along_axis(comb, (2 * v + h) * blocks + lane // slots, axis=1)

    def rows_of(i, start):
        return jnp.concatenate([sorted_q[i, start + q] for q in range(window)], axis=0)

    def further(o, i, comb, extra):
        sims = product(o, rows_of(i, nq - window), extra)
        out = []
        for h in range(2):
            whose = spread_comb(comb, extra, h) >> 8
            out.append([chosen(part, h, whose, nq - window, None) for part in sims])
        return out

    def tile(o, i, comb, first, past, v):
        sims = product(o, rows_of(i, first[v]), v)
        out = []
        for h in range(2):
            here = spread_comb(comb, v, h)
            whose, until = here >> 8, here & 255
            mine = chosen(sims[0], h, whose, first[v], past[h][0])
            theirs = chosen(sims[1], h, whose, first[v], past[h][1])
            mine = jnp.where((position < until)[None], mine, F32(-1e30))
            theirs = jnp.where((position2 < until)[None], theirs, F32(-1e30))
            out.append(jnp.maximum(mine, theirs))
        return out

    def fold(leaf, v, dist):
        if dist == slots:
            return merge(*leaf(v), 1)
        return merge(fold(leaf, v, dist * 2), fold(leaf, v + dist // 2, dist * 2), dist)

    def put(j, value):
        best[j + 1] = value.reshape(per_query, cap)

    def kept(v):
        return raw[2 * v], raw[2 * v + 1]

    def compute(g):
        put(GROUP * g - 1, fold(kept, 0, 2))
        for i in range(GROUP):
            m, _, p, _, _ = entry(g, i)
            mixed = qall[m, p].reshape(qrows, qall.shape[4])
            query = jnp.dot(sorting[...], mixed, preferred_element_type=F32).astype(BF16)
            sorted_q[i] = query.reshape(nq, per_query, query.shape[1])
        for i in range(GROUP):
            o = entry(g, i)[4]
            comb = combs[o]
            first, extra = starts(o)
            leaf = functools.partial(tile, o, i, comb, first, further(o, i, comb, extra))
            if i < GROUP - 1:
                put(GROUP * g + i, fold(leaf, 0, 2))
            else:
                for v in range(blocks):
                    raw[2 * v], raw[2 * v + 1] = leaf(v)
        for i in range(GROUP):
            combine(entry(jnp.minimum(g + 1, groups - 1), i)[4])

    def send_best(j):
        return send(best.at[j + 1], inbox.at[j // nx, x], m_send.at[j], m_recv.at[j // nx, x], d, j % nx * 2 + c)

    def give_best(j):
        @pl.when((j >= 0) & (j % nx != x))
        def _():
            send_best(j).start()

    def target(m):
        j = x + nx * m
        o = jnp.int32(0)
        for i in range(GROUP):
            o = jnp.where(j % GROUP == i, entry(j // GROUP, i)[3], o)
        return o

    def send_sum(m, tp, o):
        return (o == d) & (tp == t), send(sums.at[m], table.at[d], t_send.at[m, tp], t_recv.at[d], o, tp)

    def reduce(m):
        total = best[x + nx * m + 1]
        for p in range(1, nx):
            src = (x + p) % nx
            send(inbox.at[m, src], inbox.at[m, src], d_send, m_recv.at[m, src], d, sibling).wait_recv()
            total = jnp.maximum(total, inbox[m, src])
        sums[m] = jnp.sum(total, axis=0, keepdims=True)
        o = target(m)

        def give(tp):
            mine, copy = send_sum(m, tp, o)

            @pl.when(mine)
            def _():
                table[d] = sums[m]

            @pl.when(jnp.logical_not(mine))
            def _():
                copy.start()

        loop(0, nt, give)

    share_docs = send(docs, docs2, d_send, d_recv, d, sibling)
    loads[3].wait()
    loads[4].wait()
    share_docs.start()
    for k in range(1, nz):
        relay(k)
        if k == 2:
            forward(0)
    for m in range(nz // 2):
        forward_list(m)
    for m in range(1, nz // 2):
        if 2 * m - 1 < len(places[1]):
            relay_rest(places[1][2 * m - 2])
            relay_rest(places[1][2 * m - 1])
        forward(m)
    for m in range(nz // 2):
        for p in range(1, ny):
            row_arrived(m, p)
    to_smem = pltpu.make_async_copy(lists_in, lists, s_sem)
    to_smem.start()
    for i in range(GROUP):
        combine(entry(0, i)[4])
    to_smem.wait()
    share_docs.wait_recv()

    summing = [(nx * (m + 1) - 1) // GROUP + LAG for m in range(no // nt)]

    def step(g):
        complete(g)
        compute(g)
        for i in range(GROUP):
            give_best(GROUP * g + i - 1)
        for m, n in enumerate(summing):
            if n < groups:
                pl.when(g == n)(functools.partial(reduce, m))

    loop(0, groups, step)
    put(no // 2 - 1, fold(kept, 0, 2))
    give_best(jnp.int32(no // 2 - 1))
    for m, n in enumerate(summing):
        if n >= groups:
            reduce(m)

    for k in range(nz):
        each_tok(k, send_tok, left)
        if along(k) % 2:
            each_tok(k, send_rest, left)
            for p in range(1, ny):
                send_piece(k, p).wait_send()
    for k in range(1, nz):
        send_z(k).wait_send()
    for m in range(nz // 2):
        for p in range(1, ny):
            pl.when(odd == 0)(lambda: send_y(m, p).wait_send())
            send_row(m, p).wait_send()
    share_docs.wait_send()
    pl.when(c == z % 2)(lambda: loop(1, nz, lambda k: send_list(k).wait_send()))

    def drained(j):
        @pl.when(j % nx != x)
        def _():
            send_best(j).wait_send()

    loop(0, no // 2, drained)

    def sums_left(i):
        mine, copy = send_sum(i // nt, i % nt, target(i // nt))

        @pl.when(jnp.logical_not(mine))
        def _():
            copy.wait_send()

    loop(0, no, sums_left)

    def score_arrived(s):
        @pl.when(jnp.logical_not((s == d) & (t == order.index((0, 0)) % nx * 2 + z % 2)))
        def _():
            send(table.at[s], table.at[s], t_send.at[0, 0], t_recv.at[s], d, sibling).wait_recv()

    loop(0, no, score_arrived)

    for s in range(no):
        table2[s : s + 1] = table[s]
    whole = table2[...]
    top = whole.astype(BF16).astype(F32)
    rest = whole - top
    middle = rest.astype(BF16).astype(F32)
    stacked = [top, middle, rest - middle]
    pad = 128 - 3 * no
    stacked.append(jnp.zeros((pad, cap), F32))
    turned = jnp.transpose(jnp.concatenate(stacked, axis=0)).astype(BF16)
    for q in range(nq):
        mine = onehots[q]
        select = jnp.concatenate([mine, mine, mine, jnp.zeros((pad, cands), BF16)], axis=0)
        found = jnp.dot(turned, select, preferred_element_type=F32)
        hit = iota((cap, cands), 0) == ranks[q]
        out_ref[q : q + 1] = jnp.sum(jnp.where(hit, found, F32(0.0)), axis=0, keepdims=True)


def on_device(ny, nz, nt, query_states, proj_weight, doc_vectors, document_token_length, candidates):
    nq, per, width = query_states.shape
    ndocs, slots, dim = doc_vectors.shape
    cands = candidates.shape[1]
    no = ny * nz
    cap = 2 * nq * cands // no
    rows = nq * per
    lanes = min(128, ndocs)
    dma = pltpu.SemaphoreType.DMA
    hbm = pl.BlockSpec(memory_space=pl.ANY)
    return pl.pallas_call(
        functools.partial(kernel, ny, nz, nt),
        out_shape=jax.ShapeDtypeStruct((nq, cands), F32),
        in_specs=[hbm] * 5,
        out_specs=pl.BlockSpec(memory_space=pltpu.VMEM),
        scratch_shapes=[
            pltpu.VMEM((ndocs, slots, dim), BF16),
            pltpu.VMEM((ndocs, slots, dim), BF16),
            pltpu.VMEM((nq, per, width), BF16),
            pltpu.VMEM((rows, width), F32),
            pltpu.VMEM((width, dim), BF16),
            pltpu.VMEM((ndocs // lanes, lanes), I32),
            pltpu.VMEM((nq, cands), I32),
            pltpu.VMEM((nz, rows, dim), BF16),
            pltpu.VMEM((nz // 2, ny, rows, dim), BF16),
            pltpu.VMEM((nz // 2, ny, nt, rows, dim), BF16),
            pltpu.VMEM((rows * nt, rows * nt), BF16),
            pltpu.VMEM((nz, ny, 1, cap), I32),
            pltpu.VMEM((nz, ny, 1, cap), I32),
            pltpu.VMEM((no // 2, 1, cap), I32),
            pltpu.SMEM((no // 2, 1, cap), I32),
            pltpu.VMEM((no // 2, 8, cap), I32),
            pltpu.VMEM((nq, no, cands), BF16),
            pltpu.VMEM((nq, 1, cands), I32),
            pltpu.VMEM((GROUP, nq, per * nt, dim), BF16),
            pltpu.VMEM((slots, per * nt // 8, 8, cap), F32),
            pltpu.VMEM((no // 2 + 1, per * nt, cap), F32),
            pltpu.VMEM((no // nt, nt // 2, per * nt, cap), F32),
            pltpu.VMEM((no // nt, 1, cap), F32),
            pltpu.VMEM((no, 1, cap), F32),
            pltpu.VMEM((no, cap), F32),
            dma((5,)),
            dma((nz, nt // 2)),
            dma((nz, nt)),
            dma((nz, nt // 2)),
            dma((nz, nt)),
            dma((nz, ny)),
            dma((nz, ny)),
            dma((nz,)),
            dma((nz,)),
            dma((nz // 2, ny)),
            dma,
            dma,
            dma((nz // 2, ny)),
            dma((nz,)),
            dma((nz,)),
            dma((nz // 2, ny)),
            dma((no // 2,)),
            dma((no // 2,)),
            dma((no // nt, nt // 2)),
            dma((no // nt, nt)),
            dma((no,)),
            dma,
        ],
        compiler_params=pltpu.CompilerParams(
            collective_id=0, has_side_effects=True, vmem_limit_bytes=60 * 2**20
        ),
    )(
        doc_vectors,
        query_states,
        proj_weight,
        document_token_length.reshape(-1, lanes),
        candidates,
    )


def solution(mesh, ny=4):
    no, nt = mesh.shape["doc"], mesh.shape["tok"]
    placed = (P("doc", "tok", None), P(), P("doc", "tok", None), P("doc"), P("doc", None))
    return jax.shard_map(
        functools.partial(on_device, ny, no // ny, nt),
        mesh=mesh, in_specs=placed, out_specs=P("doc", None), check_vma=False,
    )
```

time: 54.4 us -> 47.5 us (0.87)
  Pallas kernels: 52.9 us -> 46.1 us
    pallas_call x1, Pallas kernels: 52.9 us -> 46.1 us  [on_device(): pl.pallas_call(functools.partial(kernel, ny, nz, nt), out_shape=jax.Shape...]
where the time goes in v3:
time: 47.5 us; the launch traced here: 47.4 us
  Pallas kernels  46.1 us (97%)
  local copies, waits for them, and re-layouts  1.3 us (3%)
    pallas_call x1, Pallas kernels, on_device(): pl.pallas_call(functools.partial(kernel, ny, nz, nt), out_shape=jax.Shape...  46.1 us
    unnamed x1, local copies, waits for them, and re-layouts  1.3 us

profile of v3, /device:TPU:1, one launch (start us, length us, event | category | flops | bytes accessed | tf_op | source)
XLA Modules:
  0.0 47.4 jit_solution(2660124761932142530)
XLA Ops:
  0.0 46.1 %shard_map.55 = f32[8,256]{1,0:T(8,128)} custom-call(bf16[1024,16,128]{2,1,0:T(8,128)(2,1)} %docs_hbm.1, bf16[8,4,1024]{2,1,0:T(4,128)(2,1)} %qs_hbm.1, bf16[1024,128]{1,0:T(8,128)(2,1)} %w_hbm.1, s32[8,128]{1,0:T(8,128)} %bitcast.1, s32[8,256]{1,0:T(8,128)} %cand_hbm.1), custom_call_target="tpu_custom_call" | custom-call | tf_op jit(solution)/shard_map/pallas_call | solution.py:540
  46.1 1.3 %copy.7 = f32[8,256]{1,0:T(8,128)} copy(f32[8,256]{1,0:T(8,128)} %shard_map.55) | data formatting | bytes 16384

commit v4 on v3

--- a/solution.py
+++ b/solution.py
@@ -23,14 +23,13 @@
 
 
 def schedule(ny, nz):
-    near = [5.0 + 1.0 * m for m in range(nz // 2)]
-    entries = [(near[m] + (3.0 if p else 0.0), m, p) for m in range(nz // 2) for p in range(ny)]
-    return [(m, p) for _, m, p in sorted(entries)]
+    own = [(m, 0) for m in range(nz // 2)]
+    return own + [(m, p) for m in range(nz // 2) for p in range(1, ny)]
 
 
 def kernel(
     ny, nz, nt, docs_hbm, qs_hbm, w_hbm, len_hbm, cand_hbm, out_ref,
-    docs, docs2, qs, qrow, w, len_ref, cand_ref, ublk, pieces, qall, sorting, lists_out, lists_z, lists_in, lists, combs, onehots, ranks,
+    docs, docs2, qs, qrow, w, len_ref, cand_ref, ublk, pieces, qall, sorting, lists_out, lists_z, lists_in, near_lists, far_lists, combs, onehots, ranks,
     sorted_q, raw, best, inbox, sums, table, table2,
     in_sem, a_send, a_recv, b_send, b_recv, v_send, v_recv, z_send, z_recv, y_send, d_send, d_recv, q_recv, l_send, l_recv, yl_send, yl_recv,
     m_send, m_recv, t_send, t_recv, s_sem,
@@ -50,6 +49,7 @@
     order = schedule(ny, nz)
     groups = no // 2 // GROUP
     nx = nt // 2
+    depth = nz // 2
     x, odd = t // 2, (z + c) % 2
     places = [[k for k in range(nz) if along(k) % 2 == side] for side in (0, 1)]
 
@@ -215,7 +215,7 @@
 
     def send_row(m, p):
         o, to = owner(place(m), 0), (y + p) % ny
-        slot = m * ny + ny - p
+        slot = (ny - p) * depth + m
         return send(
             lists_z.at[o % nz, to], lists_in.at[slot], yl_send.at[m, p], yl_recv.at[slot], to * nz + z, t
         )
@@ -251,10 +251,10 @@
 
         for p in range(1, ny):
             send_row(m, p).start()
-        lists_in[m * ny] = lists_z[o % nz, y]
+        lists_in[m] = lists_z[o % nz, y]
 
     def row_arrived(m, p):
-        slot = m * ny + p
+        slot = p * depth + m
         send(lists_in.at[slot], lists_in.at[slot], d_send, yl_recv.at[slot], d, sibling).wait_recv()
 
     def entry(g, i):
@@ -264,7 +264,7 @@
             m = jnp.where(g == n, step_m, m)
             k = jnp.where(g == n, place(step_m), k)
             p = jnp.where(g == n, step_p, p)
-        return m, k, p, owner(k, p), m * ny + p
+        return m, k, p, owner(k, p), p * depth + m
 
     def complete(g):
         for i in range(GROUP):
@@ -307,7 +307,7 @@
 
     window = nq // 2
 
-    def starts(o):
+    def starts(lists, o):
         first, extra = [], jnp.int32(0)
         for v in range(blocks):
             first.append(jnp.minimum((lists[o, 0, slots * v] >> shift) & (nq - 1), nq - window))
@@ -315,7 +315,7 @@
             extra = extra + jnp.where(last - first[v] >= window, v, 0)
         return first, extra & (blocks - 1)
 
-    def product(o, query, v):
+    def product(lists, o, query, v):
         picks = [lists[o, 0, slots * v + n] & (ndocs - 1) for n in range(slots)]
         out = []
         for source in (docs, docs2):
@@ -336,16 +336,16 @@
     def rows_of(i, start):
         return jnp.concatenate([sorted_q[i, start + q] for q in range(window)], axis=0)
 
-    def further(o, i, comb, extra):
-        sims = product(o, rows_of(i, nq - window), extra)
+    def further(lists, o, i, comb, extra):
+        sims = product(lists, o, rows_of(i, nq - window), extra)
         out = []
         for h in range(2):
             whose = spread_comb(comb, extra, h) >> 8
             out.append([chosen(part, h, whose, nq - window, None) for part in sims])
         return out
 
-    def tile(o, i, comb, first, past, v):
-        sims = product(o, rows_of(i, first[v]), v)
+    def tile(lists, o, i, comb, first, past, v):
+        sims = product(lists, o, rows_of(i, first[v]), v)
         out = []
         for h in range(2):
             here = spread_comb(comb, v, h)
@@ -368,7 +368,7 @@
     def kept(v):
         return raw[2 * v], raw[2 * v + 1]
 
-    def compute(g):
+    def compute(g, lists, skipped):
         put(GROUP * g - 1, fold(kept, 0, 2))
         for i in range(GROUP):
             m, _, p, _, _ = entry(g, i)
@@ -376,10 +376,12 @@
             query = jnp.dot(sorting[...], mixed, preferred_element_type=F32).astype(BF16)
             sorted_q[i] = query.reshape(nq, per_query, query.shape[1])
         for i in range(GROUP):
-            o = entry(g, i)[4]
-            comb = combs[o]
-            first, extra = starts(o)
-            leaf = functools.partial(tile, o, i, comb, first, further(o, i, comb, extra))
+            slot = entry(g, i)[4]
+            comb = combs[slot]
+            o = slot - skipped
+            first, extra = starts(lists, o)
+            past = further(lists, o, i, comb, extra)
+            leaf = functools.partial(tile, lists, o, i, comb, first, past)
             if i < GROUP - 1:
                 put(GROUP * g + i, fold(leaf, 0, 2))
             else:
@@ -404,7 +406,11 @@
         return o
 
     def send_sum(m, tp, o):
-        return (o == d) & (tp == t), send(sums.at[m], table.at[d], t_send.at[m, tp], t_recv.at[d], o, tp)
+        return (
+            (o == d) & (tp == t),
+            send(sums.at[m], table.at[d], t_send.at[m, tp], t_recv, o, tp),
+            pltpu.make_async_copy(sums.at[m], table.at[d], t_recv),
+        )
 
     def reduce(m):
         total = best[x + nx * m + 1]
@@ -416,11 +422,11 @@
         o = target(m)
 
         def give(tp):
-            mine, copy = send_sum(m, tp, o)
+            mine, copy, keep = send_sum(m, tp, o)
 
             @pl.when(mine)
             def _():
-                table[d] = sums[m]
+                keep.start()
 
             @pl.when(jnp.logical_not(mine))
             def _():
@@ -438,33 +444,44 @@
             forward(0)
     for m in range(nz // 2):
         forward_list(m)
-    for m in range(1, nz // 2):
+    near_smem = pltpu.make_async_copy(lists_in.at[pl.ds(0, depth)], near_lists, s_sem.at[0])
+    far_smem = pltpu.make_async_copy(lists_in.at[pl.ds(depth, no // 2 - depth)], far_lists, s_sem.at[1])
+    near_smem.start()
+    for i in range(GROUP):
+        combine(entry(0, i)[4])
+
+    def step(g, lists, skipped):
+        complete(g)
+        compute(g, lists, skipped)
+        for i in range(GROUP):
+            give_best(GROUP * g + i - 1)
+
+    near_groups = depth // GROUP
+    for m in range(1, depth):
         if 2 * m - 1 < len(places[1]):
             relay_rest(places[1][2 * m - 2])
             relay_rest(places[1][2 * m - 1])
         forward(m)
-    for m in range(nz // 2):
-        for p in range(1, ny):
-            row_arrived(m, p)
-    to_smem = pltpu.make_async_copy(lists_in, lists, s_sem)
-    to_smem.start()
-    for i in range(GROUP):
-        combine(entry(0, i)[4])
-    to_smem.wait()
-    share_docs.wait_recv()
-
+        if m == depth - 1:
+            for n in range(depth):
+                for p in range(1, ny):
+                    row_arrived(n, p)
+            far_smem.start()
+        if m == GROUP - 1:
+            near_smem.wait()
+            share_docs.wait_recv()
+        if (m + 1) % GROUP == 0:
+            step(jnp.int32((m + 1) // GROUP - 1), near_lists, 0)
+    far_smem.wait()
     summing = [(nx * (m + 1) - 1) // GROUP + LAG for m in range(no // nt)]
 
-    def step(g):
-        complete(g)
-        compute(g)
-        for i in range(GROUP):
-            give_best(GROUP * g + i - 1)
+    def far_step(g):
+        step(g, far_lists, depth)
         for m, n in enumerate(summing):
             if n < groups:
                 pl.when(g == n)(functools.partial(reduce, m))
 
-    loop(0, groups, step)
+    loop(near_groups, groups, far_step)
     put(no // 2 - 1, fold(kept, 0, 2))
     give_best(jnp.int32(no // 2 - 1))
     for m, n in enumerate(summing):
@@ -494,7 +511,7 @@
     loop(0, no // 2, drained)
 
     def sums_left(i):
-        mine, copy = send_sum(i // nt, i % nt, target(i // nt))
+        mine, copy, _ = send_sum(i // nt, i % nt, target(i // nt))
 
         @pl.when(jnp.logical_not(mine))
         def _():
@@ -502,12 +519,7 @@
 
     loop(0, no, sums_left)
 
-    def score_arrived(s):
-        @pl.when(jnp.logical_not((s == d) & (t == order.index((0, 0)) % nx * 2 + z % 2)))
-        def _():
-            send(table.at[s], table.at[s], t_send.at[0, 0], t_recv.at[s], d, sibling).wait_recv()
-
-    loop(0, no, score_arrived)
+    send(table, table, d_send, t_recv, d, sibling).wait_recv()
 
     for s in range(no):
         table2[s : s + 1] = table[s]
@@ -557,7 +569,8 @@
             pltpu.VMEM((nz, ny, 1, cap), I32),
             pltpu.VMEM((nz, ny, 1, cap), I32),
             pltpu.VMEM((no // 2, 1, cap), I32),
-            pltpu.SMEM((no // 2, 1, cap), I32),
+            pltpu.SMEM((nz // 2, 1, cap), I32),
+            pltpu.SMEM((no // 2 - nz // 2, 1, cap), I32),
             pltpu.VMEM((no // 2, 8, cap), I32),
             pltpu.VMEM((nq, no, cands), BF16),
             pltpu.VMEM((nq, 1, cands), I32),
@@ -588,8 +601,8 @@
             dma((no // 2,)),
             dma((no // nt, nt // 2)),
             dma((no // nt, nt)),
-            dma((no,)),
             dma,
+            dma((2,)),
         ],
         compiler_params=pltpu.CompilerParams(
             collective_id=0, has_side_effects=True, vmem_limit_bytes=60 * 2**20

time: 47.5 us -> 45.3 us (0.954)
  Pallas kernels: 46.1 us -> 43.8 us
    pallas_call x1, Pallas kernels: 46.1 us -> 43.8 us  [on_device(): pl.pallas_call(functools.partial(kernel, ny, nz, nt), out_shape=jax.Shape...]
where the time goes in v4:
time: 45.3 us; the launch traced here: 45.1 us
  Pallas kernels  43.8 us (97%)
  local copies, waits for them, and re-layouts  1.3 us (3%)
    pallas_call x1, Pallas kernels, on_device(): pl.pallas_call(functools.partial(kernel, ny, nz, nt), out_shape=jax.Shape...  43.8 us
    unnamed x1, local copies, waits for them, and re-layouts  1.3 us

profile of v4, /device:TPU:1, one launch (start us, length us, event | category | flops | bytes accessed | tf_op | source)
XLA Modules:
  0.0 45.1 jit_solution(1263675188850208141)
XLA Ops:
  0.0 43.8 %shard_map.55 = f32[8,256]{1,0:T(8,128)} custom-call(bf16[1024,16,128]{2,1,0:T(8,128)(2,1)} %docs_hbm.1, bf16[8,4,1024]{2,1,0:T(4,128)(2,1)} %qs_hbm.1, bf16[1024,128]{1,0:T(8,128)(2,1)} %w_hbm.1, s32[8,128]{1,0:T(8,128)} %bitcast.1, s32[8,256]{1,0:T(8,128)} %cand_hbm.1), custom_call_target="tpu_custom_call" | custom-call | tf_op jit(solution)/shard_map/pallas_call | solution.py:552
  43.8 1.3 %copy.7 = f32[8,256]{1,0:T(8,128)} copy(f32[8,256]{1,0:T(8,128)} %shard_map.55) | data formatting | bytes 16384

commit v5 on v4

--- a/solution.py
+++ b/solution.py
@@ -29,7 +29,7 @@
 
 def kernel(
     ny, nz, nt, docs_hbm, qs_hbm, w_hbm, len_hbm, cand_hbm, out_ref,
-    docs, docs2, qs, qrow, w, len_ref, cand_ref, ublk, pieces, qall, sorting, lists_out, lists_z, lists_in, near_lists, far_lists, combs, onehots, ranks,
+    docs, docs2, qs, qrow, w, len_ref, cand_ref, ublk, pieces, qall, sorting, lists_out, lists_z, lists_in, near_lists, far_lists, combs, onehots, selects, ranks,
     sorted_q, raw, best, inbox, sums, table, table2,
     in_sem, a_send, a_recv, b_send, b_recv, v_send, v_recv, z_send, z_recv, y_send, d_send, d_recv, q_recv, l_send, l_recv, yl_send, yl_recv,
     m_send, m_recv, t_send, t_recv, s_sem,
@@ -190,6 +190,10 @@
     row, col = iota((qrows, qrows), 0), iota((qrows, qrows), 1)
     from_row = ((row // per) % nt) * (per * nq) + (row // per_query) * per + row % per
     sorting[...] = (from_row == col).astype(BF16)
+    pad = 128 - 3 * no
+    for q in range(nq):
+        mine = onehots[q]
+        selects[q] = jnp.concatenate([mine, mine, mine, jnp.zeros((pad, cands), BF16)], axis=0)
 
     def relay(k):
         send_z(k).wait_recv()
@@ -440,10 +444,9 @@
     share_docs.start()
     for k in range(1, nz):
         relay(k)
-        if k == 2:
-            forward(0)
     for m in range(nz // 2):
         forward_list(m)
+    forward(0)
     near_smem = pltpu.make_async_copy(lists_in.at[pl.ds(0, depth)], near_lists, s_sem.at[0])
     far_smem = pltpu.make_async_copy(lists_in.at[pl.ds(depth, no // 2 - depth)], far_lists, s_sem.at[1])
     near_smem.start()
@@ -528,13 +531,10 @@
     rest = whole - top
     middle = rest.astype(BF16).astype(F32)
     stacked = [top, middle, rest - middle]
-    pad = 128 - 3 * no
     stacked.append(jnp.zeros((pad, cap), F32))
     turned = jnp.transpose(jnp.concatenate(stacked, axis=0)).astype(BF16)
     for q in range(nq):
-        mine = onehots[q]
-        select = jnp.concatenate([mine, mine, mine, jnp.zeros((pad, cands), BF16)], axis=0)
-        found = jnp.dot(turned, select, preferred_element_type=F32)
+        found = jnp.dot(turned, selects[q], preferred_element_type=F32)
         hit = iota((cap, cands), 0) == ranks[q]
         out_ref[q : q + 1] = jnp.sum(jnp.where(hit, found, F32(0.0)), axis=0, keepdims=True)
 
@@ -573,6 +573,7 @@
             pltpu.SMEM((no // 2 - nz // 2, 1, cap), I32),
             pltpu.VMEM((no // 2, 8, cap), I32),
             pltpu.VMEM((nq, no, cands), BF16),
+            pltpu.VMEM((nq, 128, cands), BF16),
             pltpu.VMEM((nq, 1, cands), I32),
             pltpu.VMEM((GROUP, nq, per * nt, dim), BF16),
             pltpu.VMEM((slots, per * nt // 8, 8, cap), F32),

time: 45.3 us -> 45.3 us (level)
  no operation moved by 1% of the time
where the time goes in v5:
time: 45.3 us; the launch traced here: 45.1 us
  Pallas kernels  43.8 us (97%)
  local copies, waits for them, and re-layouts  1.3 us (3%)
    pallas_call x1, Pallas kernels, on_device(): pl.pallas_call(functools.partial(kernel, ny, nz, nt), out_shape=jax.Shape...  43.8 us
    unnamed x1, local copies, waits for them, and re-layouts  1.3 us

profile of v5, /device:TPU:1, one launch (start us, length us, event | category | flops | bytes accessed | tf_op | source)
XLA Modules:
  0.0 45.1 jit_solution(16374157052247330809)
XLA Ops:
  0.0 43.8 %shard_map.55 = f32[8,256]{1,0:T(8,128)} custom-call(bf16[1024,16,128]{2,1,0:T(8,128)(2,1)} %docs_hbm.1, bf16[8,4,1024]{2,1,0:T(4,128)(2,1)} %qs_hbm.1, bf16[1024,128]{1,0:T(8,128)(2,1)} %w_hbm.1, s32[8,128]{1,0:T(8,128)} %bitcast.1, s32[8,256]{1,0:T(8,128)} %cand_hbm.1), custom_call_target="tpu_custom_call" | custom-call | tf_op jit(solution)/shard_map/pallas_call | solution.py:552
  43.8 1.3 %copy.7 = f32[8,256]{1,0:T(8,128)} copy(f32[8,256]{1,0:T(8,128)} %shard_map.55) | data formatting | bytes 16384

commit v6 on v5

--- a/solution.py
+++ b/solution.py
@@ -11,7 +11,7 @@
 F32, BF16, I32 = jnp.float32, jnp.bfloat16, jnp.int32
 NT = (((1,), (1,)), ((), ()))
 GROUP = 2
-LAG = 4
+LAG = 8
 
 
 def iota(shape, dim):
@@ -436,7 +436,8 @@
             def _():
                 copy.start()
 
-        loop(0, nt, give)
+        for tp in range(nt):
+            give(tp)
 
     share_docs = send(docs, docs2, d_send, d_recv, d, sibling)
     loads[3].wait()

time: 45.3 us -> 45 us (level)
  no operation moved by 1% of the time
where the time goes in v6:
time: 45 us; the launch traced here: 44.9 us
  Pallas kernels  43.6 us (97%)
  local copies, waits for them, and re-layouts  1.3 us (3%)
    pallas_call x1, Pallas kernels, on_device(): pl.pallas_call(functools.partial(kernel, ny, nz, nt), out_shape=jax.Shape...  43.6 us
    unnamed x1, local copies, waits for them, and re-layouts  1.3 us

profile of v6, /device:TPU:1, one launch (start us, length us, event | category | flops | bytes accessed | tf_op | source)
XLA Modules:
  0.0 44.9 jit_solution(7024997243881768094)
XLA Ops:
  0.0 43.6 %shard_map.55 = f32[8,256]{1,0:T(8,128)} custom-call(bf16[1024,16,128]{2,1,0:T(8,128)(2,1)} %docs_hbm.1, bf16[8,4,1024]{2,1,0:T(4,128)(2,1)} %qs_hbm.1, bf16[1024,128]{1,0:T(8,128)(2,1)} %w_hbm.1, s32[8,128]{1,0:T(8,128)} %bitcast.1, s32[8,256]{1,0:T(8,128)} %cand_hbm.1), custom_call_target="tpu_custom_call" | custom-call | tf_op jit(solution)/shard_map/pallas_call | solution.py:553
  43.6 1.3 %copy.7 = f32[8,256]{1,0:T(8,128)} copy(f32[8,256]{1,0:T(8,128)} %shard_map.55) | data formatting | bytes 16384
